TPU v7x, 256 devices: a whole 4x4x8 slice. The times are simulated.
256 devices in a mesh: cfg: 2 (over x_lo), seq: 128 (over y, z, x_hi, core).
Axes of the slice: x: 4 (x_hi: 2, x_lo: 2; x = x_hi * 2 + x_lo), y: 4, z: 8, core: 2. Of those that a mesh axis runs over, the one named last changes fastest.
Arguments:
- coarse_hidden: bfloat16 [2, 256, 64, 2048], P('cfg', 'seq'), may hold values from -6 to 6
- coarse_modulation: float32 [2, 2, 2048], P('cfg'), may hold values from -3 to 3
- final_weight: bfloat16 [2048, 32], replicated, may hold values from -0.125 to 0.125
- coarse_latent: float32 [256, 2048], P('seq'), may hold values from -6 to 6
- step_index: int32 [1], replicated, may hold values from 0 to 49
- guide_index: int32 [1], replicated, may hold values from 0 to 4095
- guide_scales: float32 [4096], replicated, may hold values from 1.5 to 6
- upsample_weight: float32 [288, 32], replicated, may hold values from -0.375 to 0.375
- upsample_bias: float32 [32], replicated, may hold values from -3 to 3
- embed_weight: bfloat16 [32, 2048], replicated, may hold values from -1 to 1
- embed_bias: float32 [2048], replicated, may hold values from -3 to 3
- fine_modulation: float32 [3, 2048], replicated, may hold values from -3 to 3
- project_weight: bfloat16 [2048, 3072], P(('cfg', 'seq')), may hold values from -0.125 to 0.125
- query_gain: float32 [128], replicated, may hold values from 0.25 to 1.75
- key_gain: float32 [128], replicated, may hold values from 0.25 to 1.75
- text_keys: bfloat16 [256, 1024], replicated, may hold values from -6 to 6
- text_values: bfloat16 [256, 1024], replicated, may hold values from -6 to 6
- text_length: int32 [1], replicated, may hold values from 192 to 256
- output_weight: bfloat16 [1024, 2048], P(None, ('cfg', 'seq')), may hold values from -0.1875 to 0.1875
Outputs:
- guided_velocity: float32 [256, 2048], P('seq')
- fine_latent: float32 [256, 2, 4096], P('seq', 'cfg')
- fine_hidden: bfloat16 [256, 2, 128, 2048], P('seq', 'cfg')
All inputs are finite; a program needn't handle non-finite values.
Results may differ from a plain program's by a relative error of at most 0.0053.
Values may be sent and summed in bfloat16 or wider, within the bound.
A program may use at most 128 MiB of HBM per device.

v0:
```python
import jax
import jax.numpy as jnp
from jax import lax
from jax.sharding import PartitionSpec as P

HEADS = 8
STEPS = 50


epsilon = 1e-06
flow_shift = 5.0
highest = lax.Precision.HIGHEST


def from_partner(shard, axis, bit):
    return lax.ppermute(shard, axis, [(i, i ^ 1 << bit) for i in range(lax.axis_size(axis))])


def with_halo(block, sides, width):
    for axis, dim in sides:
        count = lax.axis_size(axis)
        forward = [(i, i + 1) for i in range(count - 1)]
        backward = [(target, source) for source, target in forward]
        low = lax.ppermute(
            lax.slice_in_dim(block, block.shape[dim] - width, None, axis=dim), axis, forward
        )
        high = lax.ppermute(lax.slice_in_dim(block, 0, width, axis=dim), axis, backward)
        block = jnp.concatenate([low, block, high], axis=dim)
    return block


def layer_norm(values):
    centred = values - jnp.mean(values, -1, keepdims=True)
    return centred * lax.rsqrt(jnp.mean(centred * centred, -1, keepdims=True) + epsilon)


def rms_heads(values, gain_vector, head_width):
    shaped = values.reshape(values.shape[0], -1, head_width)
    scaled = (
        shaped * lax.rsqrt(jnp.mean(shaped * shaped, -1, keepdims=True) + epsilon) * gain_vector
    )
    return scaled.reshape(values.shape[0], -1)


def sigma_at(step_value):
    fraction = 1.0 - step_value.astype(jnp.float32) / STEPS
    return flow_shift * fraction / (1.0 + (flow_shift - 1.0) * fraction)


def pick_scale(scale_table, slot_index):
    slots = jnp.arange(scale_table.shape[0], dtype=jnp.int32)
    return jnp.sum(jnp.where(slots == slot_index, scale_table, 0.0))


def attend(queries, image_keys, image_values, text_keys, text_values, image_mask, text_mask, heads):
    head_width = queries.shape[1] // heads
    score_scale = head_width ** (-0.5)
    dims = (((1,), (1,)), ((), ()))

    def one_head(head_index):
        column_start = head_index * head_width
        query_part = lax.dynamic_slice_in_dim(queries, column_start, head_width, 1)
        key_part = lax.dynamic_slice_in_dim(image_keys, column_start, head_width, 1)
        value_part = lax.dynamic_slice_in_dim(image_values, column_start, head_width, 1)
        text_key_part = lax.dynamic_slice_in_dim(text_keys, column_start, head_width, 1)
        text_value_part = lax.dynamic_slice_in_dim(text_values, column_start, head_width, 1)
        image_scores = (
            lax.dot_general(query_part, key_part, dims, preferred_element_type=jnp.float32)
            * score_scale
        )
        text_scores = (
            lax.dot_general(query_part, text_key_part, dims, preferred_element_type=jnp.float32)
            * score_scale
        )
        image_weights = jnp.where(image_mask, jnp.exp(image_scores), 0.0)
        text_weights = jnp.where(text_mask, jnp.exp(text_scores), 0.0)
        denominator = jnp.sum(image_weights, 1, keepdims=True) + jnp.sum(
            text_weights, 1, keepdims=True
        )
        image_weights = (image_weights / denominator).astype(jnp.bfloat16)
        text_weights = (text_weights / denominator).astype(jnp.bfloat16)
        return jnp.dot(image_weights, value_part, preferred_element_type=jnp.float32) + jnp.dot(
            text_weights, text_value_part, preferred_element_type=jnp.float32
        )

    stacked = lax.map(one_head, jnp.arange(heads, dtype=jnp.int32))
    return stacked.transpose(1, 0, 2).reshape(queries.shape[0], -1).astype(jnp.bfloat16)


def conv_rows(above, centre, below, upsample_weight, upsample_bias):
    tap_list = []
    for row_set in (above, centre, below):
        breadth = row_set.shape[1]
        padded = jnp.pad(row_set, ((0, 0), (1, 1), (0, 0)))
        for col_shift in range(3):
            tap_list.append(padded[:, col_shift : col_shift + breadth])
    patches = jnp.concatenate(tap_list, -1)
    flat_patches = patches.reshape(-1, patches.shape[-1])
    product = jnp.dot(flat_patches, upsample_weight, precision=highest).reshape(centre.shape)
    return product + upsample_bias + centre


def per_device(
    coarse_hidden,
    coarse_modulation,
    final_weight,
    coarse_latent,
    step_index,
    guide_index,
    guide_scales,
    upsample_weight,
    upsample_bias,
    embed_weight,
    embed_bias,
    fine_modulation,
    project_weight,
    query_gain,
    key_gain,
    text_keys,
    text_values,
    text_length,
    output_weight,
):
    row_count = coarse_hidden.shape[1]
    row_cells = coarse_hidden.shape[2]
    model_width = coarse_hidden.shape[3]
    channels = final_weight.shape[1]
    head_width = query_gain.shape[0]
    inner = project_weight.shape[1] // 3
    reach = max(row_count // 2, 1)
    branch = lax.axis_index("cfg")
    seq_index = lax.axis_index("seq")
    normed = layer_norm(coarse_hidden[0].astype(jnp.float32))
    modulated = (normed * (1.0 + coarse_modulation[0, 1]) + coarse_modulation[0, 0]).astype(
        jnp.bfloat16
    )
    velocity = jnp.dot(
        modulated.reshape(row_count * row_cells, model_width),
        final_weight,
        preferred_element_type=jnp.float32,
    ).reshape(row_count, row_cells * channels)
    partner = from_partner(velocity, "cfg", 0)
    conditional = jnp.where(branch == 0, velocity, partner)
    unconditional = jnp.where(branch == 0, partner, velocity)
    guidance = pick_scale(guide_scales, guide_index[0])
    guided = unconditional + guidance * (conditional - unconditional)
    stepped = coarse_latent + (sigma_at(step_index[0] + 1) - sigma_at(step_index[0])) * guided

    def embed_rows(grid_rows):
        grid_tokens = grid_rows.reshape(-1, channels).astype(jnp.bfloat16)
        state = jnp.dot(grid_tokens, embed_weight, preferred_element_type=jnp.float32) + embed_bias
        normed_state = (layer_norm(state) * (1.0 + fine_modulation[1]) + fine_modulation[0]).astype(
            jnp.bfloat16
        )
        return (state, normed_state)

    latent_grid = stepped.reshape(row_count, row_cells, channels)
    rim_width = reach + 1
    rimmed = with_halo(latent_grid, (("seq", 0),), rim_width)
    upsampled = jnp.repeat(jnp.repeat(rimmed, 2, 0), 2, 1)
    span = row_count + 2 * reach
    wide_grid = conv_rows(
        upsampled[1 : 1 + 2 * span],
        upsampled[2 : 2 + 2 * span],
        upsampled[3 : 3 + 2 * span],
        upsample_weight,
        upsample_bias,
    )
    grouped = wide_grid.reshape(span, 2, 2 * row_cells, channels)
    fine_grid = lax.dynamic_index_in_dim(
        grouped[reach : reach + row_count], branch, 1, keepdims=False
    )
    fine_state, fine_normed = embed_rows(fine_grid)

    def normed_rows(grid_rows):
        return embed_rows(grid_rows)[1]

    key_normed = lax.map(normed_rows, wide_grid.reshape(span, 4 * row_cells, channels)).reshape(
        -1, model_width
    )
    token_count = fine_normed.shape[0]
    weight_piece = lax.all_gather(project_weight, ("cfg", "seq"), axis=0, tiled=True)
    query_sum = jnp.dot(fine_normed, weight_piece[:, :inner], preferred_element_type=jnp.float32)
    key_sum = jnp.dot(
        key_normed, weight_piece[:, inner : 2 * inner], preferred_element_type=jnp.float32
    )
    value_sum = jnp.dot(
        key_normed, weight_piece[:, 2 * inner :], preferred_element_type=jnp.float32
    )
    queries = rms_heads(query_sum, query_gain, head_width).astype(jnp.bfloat16)
    keys = rms_heads(key_sum, key_gain, head_width).astype(jnp.bfloat16)
    values = value_sum.astype(jnp.bfloat16)
    image_keys, image_values = (keys, values)
    normed_text_keys = rms_heads(text_keys.astype(jnp.float32), key_gain, head_width).astype(
        jnp.bfloat16
    )
    key_count = image_keys.shape[0]
    query_rows = jnp.arange(token_count, dtype=jnp.int32) // (2 * row_cells)
    key_rows = jnp.arange(key_count, dtype=jnp.int32) // (4 * row_cells)
    distance = key_rows[None, :] - query_rows[:, None]
    global_rows = seq_index * row_count + key_rows - reach
    row_valid = (global_rows >= 0) & (global_rows < row_count * lax.axis_size("seq"))
    image_mask = (distance >= 0) & (distance <= 2 * reach) & row_valid[None, :]
    text_mask = (jnp.arange(text_keys.shape[0], dtype=jnp.int32) < text_length[0])[None, :]
    attended = attend(
        queries,
        image_keys,
        image_values,
        normed_text_keys,
        text_values,
        image_mask,
        text_mask,
        HEADS,
    )
    output_part = jnp.dot(
        attended,
        lax.all_gather(output_weight, ("cfg", "seq"), axis=1, tiled=True),
        preferred_element_type=jnp.float32,
    )
    fine_hidden = (fine_state + fine_modulation[2] * output_part).astype(jnp.bfloat16)
    fine_hidden = fine_hidden.reshape(row_count, 1, 2 * row_cells, model_width)
    fine_latent = fine_grid.reshape(row_count, 1, 2 * row_cells * channels)
    return (guided, fine_latent, fine_hidden)


def solution(mesh):
    placed = (
        P("cfg", "seq", None, None),
        P("cfg", None, None),
        P(),
        P("seq", None),
        P(),
        P(),
        P(),
        P(),
        P(),
        P(),
        P(),
        P(),
        P(("cfg", "seq"), None),
        P(),
        P(),
        P(),
        P(),
        P(),
        P(None, ("cfg", "seq")),
    )
    return jax.shard_map(
        per_device,
        mesh=mesh,
        in_specs=placed,
        out_specs=(P("seq", None), P("seq", "cfg", None), P("seq", "cfg", None, None)),
        check_vma=False,
    )
```

profile of v0, /device:TPU:1, one launch (start us, length us, event | category | flops | bytes accessed | tf_op | source)
XLA Modules:
  0.0 862.7 jit_solution(4221278181841568020)
XLA Ops:
  13.4 2.1 collective-permute-start
  21.4 5.2 collective-permute-start.1
  26.7 1.9 collective-permute-start.2
  28.6 5.1 collective-permute-done.2
  37.0 9.6 %while.21 = (s32[]{:T(128)}, bf16[4,256,2048]{2,1,0:T(8,128)(2,1)}, bf16[4,256,32]{2,1,0:T(8,128)(2,1)S(1)}, bf16[32,2048]{1,0:T(8,128)(2,1)S(1)}, f32[2048]{0:T(1024)S(1)}, /*index=5*/f32[3,2048]{1,0:T(4,128)S(1)}, s32[]{:T(128)}) while((s32[]{:T(128)}, bf16[4,256,2048]{2,1,0:T(8,128)(2,1)}, bf16[4,256,32]{2,1,0:T(8,128)(2,1)S(1)}, ...), condition=%wide.region_9.10_spmd, body=%wide.region_6.9_spmd.sunk | while | flops 38799616 | bytes 7603793 | solution.py:178
  48.4 389.5 %all-gather.3.cloned.1.call-done = bf16[2048,3072]{1,0:T(8,128)(2,1)} async-done(((bf16[8,3072]{1,0:T(8,128)(2,1)}), bf16[2048,3072]{1,0:T(8,128)(2,1)}) %all-gather.3.cloned.1.call-update) | async-done | bytes 12582928 | tf_op jit(solution)/shard_map/all_gather | solution.py:182
  438.0 4.6 slice_bitcast_fusion
  442.6 6.5 copy.109
  449.1 10.0 %multiply_reduce_fusion.1 = (f32[1024,8]{0,1:T(8,128)S(1)}, f32[1024,8,128]{0,2,1:T(8,128)}) fusion(bf16[1024,2048,1]{1,0,2:T(8,128)(2,1)} %bitcast.23, bf16[8,128,2048]{2,1,0:T(8,128)(2,1)} %bitcast.120), kind=kOutput, calls=%fused_computation.46 | convolution fusion | flops 4297056256 | bytes 12615680 | tf_op jit(solution)/shard_map/dot_general | solution.py:184
  459.1 3.5 fusion.29
  463.9 1.6 reduce_sum.113
  465.6 4.3 multiply_convert_fusion
  471.4 9.4 %fusion.33 = bf16[1024,1024]{1,0:T(8,128)(2,1)} fusion(bf16[1024,2048]{1,0:T(8,128)(2,1)} %bitcast.22, bf16[2048,3072]{1,0:T(8,128)(2,1)} %all-gather.3.cloned.1.call-done), kind=kOutput, calls=%fused_computation.53 | convolution fusion | flops 4296015872 | bytes 10485760 | tf_op jit(solution)/shard_map/dot_general | solution.py:187
  480.8 57.2 %while.22 = (s32[]{:T(128)}, bf16[8,256,128]{1,2,0:T(8,128)(2,1)S(1)}, s32[8]{0:T(128)S(1)}, bf16[256,1024]{1,0:T(8,128)(2,1)}, bf16[1024,1024]{0,1:T(8,128)(2,1...) while((s32[]{:T(128)}, ...), condition=%wide.region_15.16_spmd.clone, body=%wide.region_12.15_spmd.clone.sunk | while | flops 170786816 | bytes 4013791 | solution.py:86
  481.9 1.6 fusion.97
  489.1 1.6 fusion.97
  496.2 1.6 fusion.97
  503.4 1.6 fusion.97
  510.5 1.6 fusion.97
  517.7 1.6 fusion.97
  524.8 1.6 fusion.97
  532.0 1.6 fusion.97
  537.9 313.5 %all-gather.5.cloned.1.call-done = bf16[1024,2048]{0,1:T(8,128)(2,1)} async-done(((bf16[1024,8]{0,1:T(8,128)(2,1)}), bf16[1024,2048]{0,1:T(8,128)(2,1)}) %all-gather.5.cloned.1.call-update) | async-done | bytes 4194320 | tf_op jit(solution)/shard_map/all_gather | solution.py:217
  851.4 4.5 fusion.32
  (193 shorter events, 66.6 us)
Async XLA Ops:
  7.2 5.8 copy-start
  7.2 9.0 %copy-start.3 = (f32[3,2048]{1,0:T(4,128)S(1)}, f32[3,2048]{1,0:T(4,128)}, u32[]{:S(2)}) copy-start(f32[3,2048]{1,0:T(4,128)} %param.34) | copy-start | bytes 73732
  7.2 9.0 %copy-start.10 = (f32[128]{0:T(128)S(1)}, f32[128]{0:T(128)}, u32[]{:S(2)}) copy-start(f32[128]{0:T(128)} %param.36) | copy-start | bytes 1540
  7.2 9.0 %copy-start.2 = (bf16[256,1024]{1,0:T(8,128)(2,1)S(1)}, bf16[256,1024]{1,0:T(8,128)(2,1)}, u32[]{:S(2)}) copy-start(bf16[256,1024]{1,0:T(8,128)(2,1)} %param.38) | copy-start | bytes 1572868
  7.2 430.8 %all-gather.3.cloned.1.call-start = ((), (), s32[]{:S(2)}) async-start(), calls=%async_computation | async-start | bytes 12632064 | tf_op jit(solution)/shard_map/all_gather | solution.py:182
  7.9 843.5 %all-gather.5.cloned.1.call-start = ((), (), s32[]{:S(2)}) async-start(), calls=%async_computation.1 | async-start | bytes 4210688 | tf_op jit(solution)/shard_map/all_gather | solution.py:217
  13.4 6.7 collective-permute-start
  16.4 0.8 copy-start.8
  16.4 0.8 copy-start.6
  16.9 3.1 copy-start.7
  21.4 7.2 collective-permute-start.1
  26.7 7.1 collective-permute-start.2
  34.8 1.1 copy-start.5
  34.8 1.1 copy-start.9
  35.4 1.6 copy-start.1
  35.4 1.6 copy-start.4
  471.4 9.4 %copy-start.11 = (bf16[8,256,128]{1,2,0:T(8,128)(2,1)S(1)}, bf16[8,256,128]{1,2,0:T(8,128)(2,1)}, u32[]{:S(2)}) copy-start(bf16[8,256,128]{1,2,0:T(8,128)(2,1)} %custom-call.3) | copy-start | bytes 1572868
Sparse Core Ops, SparseCore 0:
  9.9 427.9 all-gather.2
  439.9 411.5 all-gather.4
where the time goes:
time: 865 us; the launch traced here: 863 us
  waiting for transfers between devices  709 us (82%)
  matrix products  71.9 us (8%)
  other arithmetic  28.6 us (3%)
  local copies, waits for them, and re-layouts  22.7 us (3%)
  between operations  16 us (2%)
  starting transfers between devices  9.32 us (1%)
    all_gather x1, waiting for transfers between devices, per_device(): lax.all_gather(project_weight, ('cfg', 'seq'), axis=0, tiled=True)  390 us
    all_gather x1, waiting for transfers between devices, per_device(): lax.all_gather(output_weight, ('cfg', 'seq'), axis=1, tiled=True)  313 us
  transfers between devices with their start and end apart: 5, of which 3 were waited for; matrix products, arithmetic and copies ran while one was open for 14% of the time, Pallas kernels for 0%

commit v1 on v0

--- a/solution.py
+++ b/solution.py
@@ -146,13 +146,35 @@
     guided = unconditional + guidance * (conditional - unconditional)
     stepped = coarse_latent + (sigma_at(step_index[0] + 1) - sigma_at(step_index[0])) * guided
 
+    scale = 1.0 + fine_modulation[1]
+    embed32 = embed_weight.astype(jnp.float32)
+    embed_centred = embed32 - jnp.mean(embed32, -1, keepdims=True)
+    bias_centred = embed_bias - jnp.mean(embed_bias)
+    folded_left = jnp.concatenate(
+        [embed_centred * scale, (bias_centred * scale)[None], fine_modulation[0][None]], 0
+    )
+    depth = project_weight.shape[0]
+    device = branch * lax.axis_size("seq") + seq_index
+    left_part = lax.dynamic_slice_in_dim(folded_left, device * depth, depth, 1)
+    folded = lax.psum(
+        jnp.dot(left_part, project_weight.astype(jnp.float32), precision=highest), ("cfg", "seq")
+    )
+    output_rows = lax.all_gather(output_weight.T, ("cfg", "seq"), axis=0, tiled=True)
+
     def embed_rows(grid_rows):
         grid_tokens = grid_rows.reshape(-1, channels).astype(jnp.bfloat16)
-        state = jnp.dot(grid_tokens, embed_weight, preferred_element_type=jnp.float32) + embed_bias
-        normed_state = (layer_norm(state) * (1.0 + fine_modulation[1]) + fine_modulation[0]).astype(
-            jnp.bfloat16
-        )
-        return (state, normed_state)
+        centred = (
+            jnp.dot(grid_tokens.astype(jnp.float32), embed_centred, precision=highest)
+            + bias_centred
+        )
+        rstd = lax.rsqrt(jnp.mean(centred * centred, -1, keepdims=True) + epsilon)
+        return (grid_tokens, rstd)
+
+    def project(tokens_rstd, start, stop):
+        tokens, rstd = tokens_rstd
+        part = folded[:, start:stop]
+        product = jnp.dot(tokens.astype(jnp.float32), part[:channels], precision=highest)
+        return rstd * (product + part[channels]) + part[channels + 1]
 
     latent_grid = stepped.reshape(row_count, row_cells, channels)
     rim_width = reach + 1
@@ -170,23 +192,13 @@
     fine_grid = lax.dynamic_index_in_dim(
         grouped[reach : reach + row_count], branch, 1, keepdims=False
     )
-    fine_state, fine_normed = embed_rows(fine_grid)
-
-    def normed_rows(grid_rows):
-        return embed_rows(grid_rows)[1]
-
-    key_normed = lax.map(normed_rows, wide_grid.reshape(span, 4 * row_cells, channels)).reshape(
-        -1, model_width
-    )
-    token_count = fine_normed.shape[0]
-    weight_piece = lax.all_gather(project_weight, ("cfg", "seq"), axis=0, tiled=True)
-    query_sum = jnp.dot(fine_normed, weight_piece[:, :inner], preferred_element_type=jnp.float32)
-    key_sum = jnp.dot(
-        key_normed, weight_piece[:, inner : 2 * inner], preferred_element_type=jnp.float32
-    )
-    value_sum = jnp.dot(
-        key_normed, weight_piece[:, 2 * inner :], preferred_element_type=jnp.float32
-    )
+    own = embed_rows(fine_grid)
+    fine_state = jnp.dot(own[0], embed_weight, preferred_element_type=jnp.float32) + embed_bias
+    around = embed_rows(wide_grid)
+    token_count = own[0].shape[0]
+    query_sum = project(own, 0, inner)
+    key_sum = project(around, inner, 2 * inner)
+    value_sum = project(around, 2 * inner, 3 * inner)
     queries = rms_heads(query_sum, query_gain, head_width).astype(jnp.bfloat16)
     keys = rms_heads(key_sum, key_gain, head_width).astype(jnp.bfloat16)
     values = value_sum.astype(jnp.bfloat16)
@@ -212,10 +224,8 @@
         text_mask,
         HEADS,
     )
-    output_part = jnp.dot(
-        attended,
-        lax.all_gather(output_weight, ("cfg", "seq"), axis=1, tiled=True),
-        preferred_element_type=jnp.float32,
+    output_part = lax.dot_general(
+        attended, output_rows, (((1,), (1,)), ((), ())), preferred_element_type=jnp.float32
     )
     fine_hidden = (fine_state + fine_modulation[2] * output_part).astype(jnp.bfloat16)
     fine_hidden = fine_hidden.reshape(row_count, 1, 2 * row_cells, model_width)

time: 865 us -> 698 us (0.81)
  waiting for transfers between devices: 709 us -> 570 us
  matrix products: 71.9 us -> 55 us
  other arithmetic: 28.6 us -> 18.2 us
    all_gather x2 -> x1, waiting for transfers between devices: 703 us -> 343 us  [per_device(): lax.all_gather(output_weight.T, ('cfg', 'seq'), axis=0, tiled=True)]
    psum x0 -> x1, waiting for transfers between devices: none -> 222 us  [per_device(): lax.psum(jnp.dot(left_part, project_weight.astype(jnp.float32), precision...]
    dot_general x2 -> x0, local copies, waits for them, and re-layouts: 11.1 us -> none  [per_device(): jnp.dot(key_normed, weight_piece[:, inner:2 * inner], preferred_element_t...]
    dot_general x9 -> x8, matrix products: 29.8 us -> 22.2 us  [the longest x3 9.39 us: project(): jnp.dot(tokens.astype(jnp.float32), part[:channels], precision=highest)]
  transfers between devices with their start and end apart: 5 -> 5, of which waited for: 3 -> 3; matrix products, arithmetic and copies ran while one was open for 14% -> 12% of each run, Pallas kernels for 0% -> 0%
where the time goes in v1:
time: 698 us; the launch traced here: 696 us
  waiting for transfers between devices  570 us (82%)
  matrix products  55 us (8%)
  local copies, waits for them, and re-layouts  21.8 us (3%)
  other arithmetic  18.2 us (3%)
  between operations  16.7 us (2%)
  starting transfers between devices  9.32 us (1%)
    all_gather x1, waiting for transfers between devices, per_device(): lax.all_gather(output_weight.T, ('cfg', 'seq'), axis=0, tiled=True)  343 us
    psum x1, waiting for transfers between devices, per_device(): lax.psum(jnp.dot(left_part, project_weight.astype(jnp.float32), precision...  222 us
  transfers between devices with their start and end apart: 5, of which 3 were waited for; matrix products, arithmetic and copies ran while one was open for 12% of the time, Pallas kernels for 0%

profile of v1, /device:TPU:1, one launch (start us, length us, event | category | flops | bytes accessed | tf_op | source)
XLA Modules:
  0.0 695.9 jit_solution(8204464123050728577)
XLA Ops:
  7.3 1.5 fusion.84
  13.5 2.0 fusion.65
  17.0 2.1 collective-permute-start
  25.4 5.2 collective-permute-start.1
  31.2 1.9 collective-permute-start.2
  33.2 5.2 collective-permute-done.2
  43.5 4.5 multiply_reduce_fusion
  48.0 221.7 %all-reduce.5.cloned.1.call-done = f32[34,3072]{1,0:T(8,128)} async-done(((f32[34,3072]{1,0:T(8,128)}), f32[34,3072]{1,0:T(8,128)}) %all-reduce.5.cloned.1.call-update) | async-done | bytes 417808 | tf_op jit(solution)/shard_map/psum | solution.py:159
  270.5 1.6 fusion.30
  273.0 3.4 bitcast_reduce_fusion
  278.3 4.4 add_convert_fusion
  283.2 58.2 %while.11 = (s32[]{:T(128)}, bf16[8,256,128]{1,2,0:T(8,128)(2,1)}, s32[8]{0:T(128)}, bf16[256,1024]{1,0:T(8,128)(2,1)S(1)}, bf16[1024,1024]{0,1:T(8,128)(2,1)S(1...) while((s32[]{:T(128)}, bf16[8,256,128]{1,2,0:T(8,128)(2,1)}, ...), condition=%wide.region_14.15_spmd.clone, body=%wide.region_11.14_spmd.clone.sunk | while | flops 170786816 | bytes 4014055 | solution.py:86
  288.4 1.3 fusion.104
  295.6 1.3 fusion.104
  302.9 1.3 fusion.104
  307.8 1.3 fusion.102
  310.2 1.3 fusion.104
  317.5 1.3 fusion.104
  324.7 1.3 fusion.104
  332.0 1.3 fusion.104
  339.3 1.3 fusion.104
  341.4 342.6 %all-gather.2.cloned.1.call-done = bf16[2048,1024]{1,0:T(8,128)(2,1)} async-done(((bf16[8,1024]{1,0:T(8,128)(2,1)}), bf16[2048,1024]{1,0:T(8,128)(2,1)}) %all-gather.2.cloned.1.call-update) | async-done | bytes 4194320 | tf_op jit(solution)/shard_map/all_gather | solution.py:162
  684.0 3.6 convolution_multiply_fusion.2
  687.6 1.4 fusion.27
  (177 shorter events, 60.7 us)
Async XLA Ops:
  7.2 9.5 %copy-start = (bf16[2048,32]{0,1:T(8,128)(2,1)S(1)}, bf16[2048,32]{0,1:T(8,128)(2,1)}, u32[]{:S(2)}) copy-start(bf16[2048,32]{0,1:T(8,128)(2,1)} %param.23) | copy-start | bytes 393220
  7.2 8.4 %copy-start.1 = (bf16[1,2,64,2048]{3,2,1,0:T(8,128)(2,1)S(1)}, bf16[1,2,64,2048]{3,2,1,0:T(8,128)(2,1)}, u32[]{:S(2)}) copy-start(bf16[1,2,64,2048]{3,2,1,0:T(8,128)(2,1)} %param.21) | copy-start | bytes 1572868
  7.2 8.9 %copy-start.8 = (f32[1,2,2048]{2,1,0:T(2,128)S(1)}, f32[1,2,2048]{2,1,0:T(2,128)}, u32[]{:S(2)}) copy-start(f32[1,2,2048]{2,1,0:T(2,128)} %param.22) | copy-start | bytes 49156
  7.2 262.5 %all-reduce.5.cloned.1.call-start = ((), (), s32[]{:S(2)}) async-start(), calls=%async_computation | async-start | bytes 983040 | tf_op jit(solution)/shard_map/psum | solution.py:159
  13.4 7.0 %copy-start.12 = (f32[128]{0:T(128)S(1)}, f32[128]{0:T(128)}, u32[]{:S(2)}) copy-start(f32[128]{0:T(128)} %param.34) | copy-start | bytes 1540
  13.5 7.0 %copy-start.13 = (f32[128]{0:T(128)S(1)}, f32[128]{0:T(128)}, u32[]{:S(2)}) copy-start(f32[128]{0:T(128)} %param.35) | copy-start | bytes 1540
  13.5 7.0 %copy-start.2 = (bf16[256,1024]{1,0:T(8,128)(2,1)S(1)}, bf16[256,1024]{1,0:T(8,128)(2,1)}, u32[]{:S(2)}) copy-start(bf16[256,1024]{1,0:T(8,128)(2,1)} %param.36) | copy-start | bytes 1572868
  15.5 668.5 %all-gather.2.cloned.1.call-start = ((), (), s32[]{:S(2)}) async-start(), calls=%async_computation.1 | async-start | bytes 4210688 | tf_op jit(solution)/shard_map/all_gather | solution.py:162
  17.0 7.0 %collective-permute-start = (f32[2,2048]{1,0:T(2,128)S(1)}, f32[2,2048]{1,0:T(2,128)S(1)}, u32[]{:S(2)}, u32[]{:S(2)}) collective-permute-start(f32[2,2048]{1,0:T(2,128)S(1)} %reshape.229), channel_id=1, source_target_pairs={{0,128},{128,0},{1,129},{129,1},{2,130},{130,2},{3,131},{131,3},{4... | collective-permute-start | bytes 49160 | tf_op jit(solution)/shard_map/ppermute | solution.py:16
  20.6 0.8 copy-start.9
  21.2 2.9 copy-start.10
  25.4 7.7 %collective-permute-start.1 = (f32[2,64,32]{2,1,0:T(8,128)S(1)}, f32[2,64,32]{2,1,0:T(8,128)S(1)}, u32[]{:S(2)}, u32[]{:S(2)}) collective-permute-start(f32[2,64,32]{2,1,0:T(8,128)S(1)} %reshape.230), channel_id=1, source_target_pairs={{0,1},{1,2},{2,3},{3,4},{4,5},{5,6},{6,7},{7,8},{8,9},{9,10},{10,1... | collective-permute-start | bytes 49160 | tf_op jit(solution)/shard_map/ppermute | solution.py:24
  31.2 7.1 %collective-permute-start.2 = (f32[2,64,32]{2,1,0:T(8,128)S(1)}, f32[2,64,32]{2,1,0:T(8,128)S(1)}, u32[]{:S(2)}, u32[]{:S(2)}) collective-permute-start(f32[2,64,32]{2,1,0:T(8,128)S(1)} %reshape.230), channel_id=1, source_target_pairs={{1,0},{2,1},{3,2},{4,3},{5,4},{6,5},{7,6},{8,7},{9,8},{10,9},{11,1... | collective-permute-start | bytes 49160 | tf_op jit(solution)/shard_map/ppermute | solution.py:27
  39.3 1.1 copy-start.7
  39.3 1.1 copy-start.11
  40.0 2.3 copy-start.3
  41.4 231.6 %copy-start.5 = (bf16[8,4,8,128]{3,2,1,0:T(8,128)(2,1)}, bf16[8,4,8,128]{3,2,1,0:T(8,128)(2,1)S(1)}, u32[]{:S(2)}) copy-start(bf16[8,4,8,128]{3,2,1,0:T(8,128)(2,1)S(1)} %convert_bitcast_fusion) | copy-start | bytes 196612
  277.2 1.1 copy-start.6
  684.0 3.6 copy-start.4
Sparse Core Ops, SparseCore 0:
  15.6 253.9 all-reduce.4
  271.6 412.4 all-gather.1

commit v2 on v1

--- a/solution.py
+++ b/solution.py
@@ -1,6 +1,8 @@
 import jax
 import jax.numpy as jnp
 from jax import lax
+from jax.experimental import pallas as pl
+from jax.experimental.pallas import tpu as pltpu
 from jax.sharding import PartitionSpec as P
 
 HEADS = 8
@@ -10,6 +12,270 @@
 epsilon = 1e-06
 flow_shift = 5.0
 highest = lax.Precision.HIGHEST
+
+
+MESH = pl.DeviceIdType.MESH
+
+
+def remote(src, dst, send_sem, recv_sem, device):
+    return pltpu.make_async_remote_copy(
+        src_ref=src, dst_ref=dst, send_sem=send_sem, recv_sem=recv_sem,
+        device_id=device, device_id_type=MESH,
+    )
+
+
+class Place:
+    def __init__(self):
+        self.x_lo = lax.axis_index("cfg")
+        seq = lax.axis_index("seq")
+        self.seq = seq
+        self.core = lax.rem(seq, 2)
+        self.x_hi = lax.rem(lax.div(seq, 2), 2)
+        self.z = lax.rem(lax.div(seq, 4), 8)
+        self.y = lax.div(seq, 32)
+        self.x = self.x_hi * 2 + self.x_lo
+        self.member = self.x_lo * 4 + self.x_hi * 2 + self.core
+        self.line = lax.div(seq, 4)
+
+    def at(self, x=None, y=None, z=None, core=None):
+        x = self.x if x is None else x
+        y = self.y if y is None else y
+        z = self.z if z is None else z
+        core = self.core if core is None else core
+        return (lax.rem(x, 2), ((y * 8 + z) * 2 + lax.div(x, 2)) * 2 + core)
+
+    def member_device(self, member):
+        return (lax.div(member, 4), self.line * 4 + lax.rem(member, 4))
+
+
+def greet(place):
+    barrier = pltpu.get_barrier_semaphore()
+    partners = [place.member_device(lax.rem(place.member + d, 8)) for d in range(1, 8)]
+    partners += [place.at(y=lax.rem(place.y + d, 4)) for d in range(1, 4)]
+    partners += [place.at(z=lax.rem(place.z + d, 8)) for d in range(1, 8)]
+    for partner in partners:
+        pl.semaphore_signal(barrier, inc=1, device_id=partner, device_id_type=MESH)
+    return barrier, len(partners)
+
+
+def comm_kernel(
+    weight_ref, output_ref, embed_ref, bias_ref, modulation_ref,
+    folded_out, rows_out,
+    left, own_rows, group_rows, partial, z_parts, y_parts, folded,
+    out_chunk, out_sibling, out_rows,
+    a_send, a_recv, rz_send, rz_recv, ry_send, ry_recv, gz_send, gz_recv, gx_send, gx_recv,
+    s_send, s_recv, wz_send, wz_recv, wp_send, wp_recv, wq_send, wq_recv, ws_send, ws_recv,
+):
+    place = Place()
+    core, z, y, member = place.core, place.z, place.y, place.member
+    group_rows[...] = jnp.zeros_like(group_rows)
+    barrier, count = greet(place)
+    for part in range(8):
+        own_rows[part] = weight_ref[:, part * 384 : (part + 1) * 384].astype(jnp.float32)
+    eye = (
+        lax.broadcasted_iota(jnp.int32, (8, 8), 0) == lax.broadcasted_iota(jnp.int32, (8, 8), 1)
+    ).astype(jnp.bfloat16)
+    turned = lax.dot_general(
+        eye, output_ref[...], (((1,), (1,)), ((), ())), preferred_element_type=jnp.float32
+    )
+    out_chunk[0] = turned[:, :512]
+    out_chunk[1] = turned[:, 512:]
+    pl.semaphore_wait(barrier, count)
+    sibling = place.at(core=1 - core)
+    swap = remote(out_chunk.at[1 - core], out_sibling, s_send, s_recv, sibling)
+    swap.start()
+    quarter = lax.rem(place.line, 4)
+    spread = []
+    for d in range(1, 8):
+        target = lax.rem(member + d, 8)
+        copy = remote(
+            own_rows.at[target],
+            group_rows.at[place.x_lo, quarter, place.x_hi * 2 + core],
+            a_send.at[d], a_recv.at[d], place.member_device(target),
+        )
+        copy.start()
+        spread.append(copy)
+    group_rows[place.x_lo, quarter, place.x_hi * 2 + core] = own_rows[member]
+    embed = embed_ref[...].astype(jnp.float32)
+    scale = 1.0 + modulation_ref[1:2, :]
+    left[0:32] = (embed - jnp.mean(embed, -1, keepdims=True)) * scale
+    bias = bias_ref[...]
+    left[32:40] = jnp.concatenate(
+        [
+            (bias - jnp.mean(bias, -1, keepdims=True)) * scale,
+            modulation_ref[0:1, :],
+            jnp.zeros((6, left.shape[1]), jnp.float32),
+        ],
+        0,
+    )
+    swap.wait()
+    mine, other = out_chunk[core], out_sibling[...]
+    first = core == 0
+    out_rows[core, place.x_lo, y, z, place.x_hi] = jnp.concatenate(
+        [jnp.where(first, mine, other), jnp.where(first, other, mine)], 0
+    ).astype(jnp.bfloat16)
+    along_z = []
+    for d in range(1, 8):
+        slot = out_rows.at[core, place.x_lo, y, z, place.x_hi]
+        copy = remote(
+            slot, slot, wz_send.at[d], wz_recv.at[d], place.at(z=lax.rem(z + d, 8))
+        )
+        copy.start()
+        along_z.append(copy)
+    for copy in spread:
+        copy.wait()
+    column = pl.multiple_of(lax.div(place.line, 4) * 128, 128)
+    total = jnp.dot(
+        left[:, pl.ds(column, 128)], group_rows[0].reshape(128, 384), precision=highest
+    ) + jnp.dot(
+        left[:, pl.ds(1024 + column, 128)], group_rows[1].reshape(128, 384), precision=highest
+    )
+    for row in range(5):
+        for block in range(3):
+            partial[row * 3 + block] = total[
+                row * 8 : row * 8 + 8, block * 128 : block * 128 + 128
+            ]
+    partial[15] = jnp.zeros((8, 128), jnp.float32)
+    scatter = []
+    for d in range(1, 8):
+        target = lax.rem(z + d, 8)
+        copy = remote(
+            partial.at[pl.ds(target * 2, 2)], z_parts.at[z],
+            rz_send.at[d], rz_recv.at[d], place.at(z=target),
+        )
+        copy.start()
+        scatter.append(copy)
+    z_parts[z] = partial[pl.ds(z * 2, 2)]
+    for copy in along_z:
+        copy.wait()
+    first_at = y * (1 - core) + place.x * core
+    second_at = place.x * (1 - core) + y * core
+
+    def piece(p, q):
+        px, py = q * (1 - core) + p * core, p * (1 - core) + q * core
+        return out_rows.at[core, lax.rem(px, 2), py, :, lax.div(px, 2)]
+
+    def piece_device(p, q):
+        return place.at(x=q * (1 - core) + p * core, y=p * (1 - core) + q * core)
+
+    along_p = []
+    for d in range(1, 4):
+        slot = piece(first_at, second_at)
+        copy = remote(
+            slot, slot, wp_send.at[d], wp_recv.at[d],
+            piece_device(lax.rem(first_at + d, 4), second_at),
+        )
+        copy.start()
+        along_p.append(copy)
+    along_q = []
+
+    def send_q(e):
+        for d in range(1, 4):
+            slot = piece(lax.rem(first_at + 4 - e, 4), second_at)
+            copy = remote(
+                slot, slot, wq_send.at[e, d], wq_recv.at[e, d],
+                piece_device(first_at, lax.rem(second_at + d, 4)),
+            )
+            copy.start()
+            along_q.append(copy)
+
+    to_sibling = []
+
+    def send_sibling(e, d):
+        slot = piece(lax.rem(first_at + 4 - e, 4), lax.rem(second_at + 4 - d, 4))
+        copy = remote(slot, slot, ws_send.at[e, d], ws_recv.at[e, d], sibling)
+        copy.start()
+        to_sibling.append(copy)
+
+    send_q(0)
+    send_sibling(0, 0)
+    for copy in scatter:
+        copy.wait()
+    y_parts[y] = jnp.sum(z_parts[...], 0)
+    over_y = []
+    for d in range(1, 4):
+        copy = remote(
+            y_parts.at[y], y_parts.at[y], ry_send.at[d], ry_recv.at[d],
+            place.at(y=lax.rem(y + d, 4)),
+        )
+        copy.start()
+        over_y.append(copy)
+    for copy in over_y:
+        copy.wait()
+    folded[member, pl.ds(z * 2, 2)] = jnp.sum(y_parts[...], 0)
+    gather_z = []
+    for d in range(1, 8):
+        slot = folded.at[member, pl.ds(z * 2, 2)]
+        copy = remote(slot, slot, gz_send.at[d], gz_recv.at[d], place.at(z=lax.rem(z + d, 8)))
+        copy.start()
+        gather_z.append(copy)
+    for e in range(1, 4):
+        along_p[e - 1].wait()
+        send_q(e)
+        send_sibling(e, 0)
+    for copy in gather_z:
+        copy.wait()
+    gather_x = []
+    for d in range(1, 8):
+        slot = folded.at[member]
+        copy = remote(
+            slot, slot, gx_send.at[d], gx_recv.at[d],
+            place.member_device(lax.rem(member + d, 8)),
+        )
+        copy.start()
+        gather_x.append(copy)
+    for copy in gather_x:
+        copy.wait()
+    for e in range(4):
+        for d in range(1, 4):
+            along_q[e * 3 + d - 1].wait()
+            send_sibling(e, d)
+    for copy in to_sibling:
+        copy.wait()
+    folded_out[...] = folded[...]
+    rows_out[...] = out_rows[...]
+
+
+def gather_parts(project_weight, output_weight, embed_weight, embed_bias, fine_modulation):
+    dma = pltpu.SemaphoreType.DMA
+    pairs = [(8,), (8,), (4,), (8,), (8,)]
+    sems = []
+    for shape in pairs:
+        sems += [dma(shape), dma(shape)]
+    sems += [dma, dma]
+    for shape in [(8,), (4,), (4, 4), (4, 4)]:
+        sems += [dma(shape), dma(shape)]
+    vmem = pl.BlockSpec(memory_space=pltpu.VMEM)
+    rows_shape = (2, 2, 4, 8, 2, 16, 512)
+    folded, rows = pl.pallas_call(
+        comm_kernel,
+        out_shape=(
+            jax.ShapeDtypeStruct((8, 16, 8, 128), jnp.float32),
+            jax.ShapeDtypeStruct(rows_shape, jnp.bfloat16),
+        ),
+        in_specs=[vmem] * 5,
+        out_specs=(vmem, vmem),
+        scratch_shapes=[
+            pltpu.VMEM((40, 2048), jnp.float32),
+            pltpu.VMEM((8, 8, 384), jnp.float32),
+            pltpu.VMEM((2, 4, 4, 8, 384), jnp.float32),
+            pltpu.VMEM((16, 8, 128), jnp.float32),
+            pltpu.VMEM((8, 2, 8, 128), jnp.float32),
+            pltpu.VMEM((4, 2, 8, 128), jnp.float32),
+            pltpu.VMEM((8, 16, 8, 128), jnp.float32),
+            pltpu.VMEM((2, 8, 512), jnp.float32),
+            pltpu.VMEM((8, 512), jnp.float32),
+            pltpu.VMEM(rows_shape, jnp.bfloat16),
+        ] + sems,
+        compiler_params=pltpu.CompilerParams(
+            collective_id=0, has_side_effects=True, vmem_limit_bytes=48 * 1024 * 1024
+        ),
+    )(project_weight, output_weight, embed_weight, embed_bias[None], fine_modulation)
+    matrix = (
+        folded[:, :15].reshape(8, 5, 3, 8, 128).transpose(1, 3, 0, 2, 4).reshape(40, 3072)
+    )
+    output_rows = rows.transpose(1, 2, 3, 4, 5, 0, 6).reshape(2048, 1024)
+    return matrix, output_rows
 
 
 def from_partner(shard, axis, bit):
@@ -146,20 +412,12 @@
     guided = unconditional + guidance * (conditional - unconditional)
     stepped = coarse_latent + (sigma_at(step_index[0] + 1) - sigma_at(step_index[0])) * guided
 
-    scale = 1.0 + fine_modulation[1]
     embed32 = embed_weight.astype(jnp.float32)
     embed_centred = embed32 - jnp.mean(embed32, -1, keepdims=True)
     bias_centred = embed_bias - jnp.mean(embed_bias)
-    folded_left = jnp.concatenate(
-        [embed_centred * scale, (bias_centred * scale)[None], fine_modulation[0][None]], 0
-    )
-    depth = project_weight.shape[0]
-    device = branch * lax.axis_size("seq") + seq_index
-    left_part = lax.dynamic_slice_in_dim(folded_left, device * depth, depth, 1)
-    folded = lax.psum(
-        jnp.dot(left_part, project_weight.astype(jnp.float32), precision=highest), ("cfg", "seq")
-    )
-    output_rows = lax.all_gather(output_weight.T, ("cfg", "seq"), axis=0, tiled=True)
+    folded, output_rows = gather_parts(
+        project_weight, output_weight, embed_weight, embed_bias, fine_modulation
+    )
 
     def embed_rows(grid_rows):
         grid_tokens = grid_rows.reshape(-1, channels).astype(jnp.bfloat16)

time: 698 us -> 182 us (0.26)
  waiting for transfers between devices: 570 us -> 4.42 us
  Pallas kernels: 0 us -> 46.7 us
  between operations: 16.7 us -> 3.41 us
  local copies, waits for them, and re-layouts: 21.8 us -> 34.5 us
    all_gather x1 -> x0, waiting for transfers between devices: 343 us -> none  [per_device(): lax.all_gather(output_weight.T, ('cfg', 'seq'), axis=0, tiled=True)]
    psum x1 -> x0, waiting for transfers between devices: 222 us -> none  [per_device(): lax.psum(jnp.dot(left_part, project_weight.astype(jnp.float32), precision...]
    pallas_call x0 -> x1, Pallas kernels: none -> 46.7 us  [gather_parts(): pl.pallas_call(comm_kernel, out_shape=(jax.ShapeDtypeStruct((8, 16, 8, 12...]
    transpose x0 -> x1, local copies, waits for them, and re-layouts: none -> 10.7 us  [gather_parts(): output_rows = rows.transpose(1, 2, 3, 4, 5, 0, 6).reshape(2048, 1024)]
  transfers between devices with their start and end apart: 5 -> 3, of which waited for: 3 -> 1; matrix products, arithmetic and copies ran while one was open for 12% -> 11% of each run, Pallas kernels for 0% -> 26%
where the time goes in v2:
time: 182 us; the launch traced here: 178 us
  matrix products  58.3 us (32%)
  Pallas kernels  46.7 us (26%)
  local copies, waits for them, and re-layouts  34.5 us (19%)
  other arithmetic  18.3 us (10%)
  starting transfers between devices  6.84 us (4%)
  loops' own time  5.72 us (3%)
  waiting for transfers between devices  4.42 us (2%)
  between operations  3.41 us (2%)
    pallas_call x1, Pallas kernels, gather_parts(): pl.pallas_call(comm_kernel, out_shape=(jax.ShapeDtypeStruct((8, 16, 8, 12...  46.7 us
    dot_general x8, matrix products, one_head(): lax.dot_general(query_part, key_part, dims, preferred_element_type=jnp.fl...  11.8 us
    transpose x1, local copies, waits for them, and re-layouts, gather_parts(): output_rows = rows.transpose(1, 2, 3, 4, 5, 0, 6).reshape(2048, 1024)  10.7 us
    dot_general x8, matrix products, one_head(): jnp.dot(image_weights, value_part, preferred_element_type=jnp.float32)  10.6 us
    dot_general x8, matrix products, one_head(): lax.dot_general(query_part, text_key_part, dims, preferred_element_type=j...  8.8 us
    dot_general x8, matrix products, one_head(): jnp.dot(text_weights, text_value_part, preferred_element_type=jnp.float32)  8.66 us
    dot_general x3, matrix products, project(): jnp.dot(tokens.astype(jnp.float32), part[:channels], precision=highest)  6.68 us
    unnamed x65, local copies, waits for them, and re-layouts  6.65 us
  transfers between devices with their start and end apart: 3, of which 1 were waited for; matrix products, arithmetic and copies ran while one was open for 11% of the time, Pallas kernels for 26%

profile of v2, /device:TPU:1, one launch (start us, length us, event | category | flops | bytes accessed | tf_op | source)
XLA Modules:
  0.0 178.2 jit_solution(13278636015976096754)
XLA Ops:
  4.2 1.4 fusion.42
  6.1 2.1 %collective-permute-start = (f32[2,2048]{1,0:T(2,128)S(1)}, f32[2,2048]{1,0:T(2,128)S(1)}, u32[]{:S(2)}, u32[]{:S(2)}) collective-permute-start(f32[2,2048]{1,0:T(2,128)S(1)} %reshape.236), channel_id=1, source_target_pairs={{0,128},{128,0},{1,129},{129,1},{2,130},{130,2},{3,131},{131,3},{4... | collective-permute-start | bytes 49160 | tf_op jit(solution)/shard_map/ppermute | solution.py:282
  11.9 46.7 %shard_map.202 = (f32[8,16,8,128]{3,2,1,0:T(8,128)S(1)}, bf16[2,2,4,8,2,16,512]{6,5,4,3,2,1,0:T(8,128)(2,1)S(1)}) custom-call(bf16[8,3072]{1,0:T(8,128)(2,1)S(1)} %copy-done.5, bf16[1024,8]{1,0:T(8,128)(2,1)S(1)} %copy.116.output_ref, bf16[32,2048]{1,0:T(8,128)(2,1)S(1)} %copy-done.2, f32[1,2048]{1,0:T(1,128)S(1)} %bitcast.121, f32[3,2048]{1,0:T(4,128)S(1)} %copy-done.4), custom_call_target="tpu_custom_call" | custom-call | tf_op jit(solution)/shard_map/pallas_call | solution.py:250
  58.6 1.9 %copy-done.1 = bf16[2,2,4,8,2,16,512]{6,5,4,3,2,1,0:T(8,128)(2,1)} copy-done((bf16[2,2,4,8,2,16,512]{6,5,4,3,2,1,0:T(8,128)(2,1)}, bf16[2,2,4,8,2,16,512]{6,5,4,3,2,1,0:T(8,128)(2,1)S(1)}, u32[]{:S(2)}) %copy-start.1) | copy-done | bytes 4194328
  65.1 2.1 %collective-permute-start.1 = (f32[2,64,32]{2,1,0:T(8,128)S(1)}, f32[2,64,32]{2,1,0:T(8,128)S(1)}, u32[]{:S(2)}, u32[]{:S(2)}) collective-permute-start(f32[2,64,32]{2,1,0:T(8,128)S(1)} %reshape.237), channel_id=1, source_target_pairs={{0,1},{1,2},{2,3},{3,4},{4,5},{5,6},{6,7},{7,8},{8,9},{9,10},{10,1... | collective-permute-start | bytes 49160 | tf_op jit(solution)/shard_map/ppermute | solution.py:290
  68.4 10.7 %copy.127 = bf16[2,4,8,2,16,2,512]{6,5,4,3,2,1,0:T(2,128)(2,1)S(1)} copy(bf16[2,4,8,2,16,2,512]{6,4,3,2,1,0,5:T(8,128)(2,1)} %bitcast.120) | data formatting | bytes 8388608 | tf_op jit(solution)/shard_map/transpose | solution.py:277
  79.1 3.1 %copy.157 = bf16[256,8,2,512]{3,1,2,0:T(8,128)(2,1)} copy(bf16[256,8,2,512]{3,2,1,0:T(2,128)(2,1)S(1)} %bitcast.122) | data formatting | bytes 8388608
  82.3 2.6 %collective-permute-start.2 = (f32[2,64,32]{2,1,0:T(8,128)S(1)}, f32[2,64,32]{2,1,0:T(8,128)S(1)}, u32[]{:S(2)}, u32[]{:S(2)}) collective-permute-start(f32[2,64,32]{2,1,0:T(8,128)S(1)} %reshape.237), channel_id=1, source_target_pairs={{1,0},{2,1},{3,2},{4,3},{5,4},{6,5},{7,6},{8,7},{9,8},{10,9},{11,1... | collective-permute-start | bytes 49160 | tf_op jit(solution)/shard_map/ppermute | solution.py:293
  84.9 4.4 %collective-permute-done.2 = f32[2,64,32]{2,1,0:T(8,128)S(1)} collective-permute-done((f32[2,64,32]{2,1,0:T(8,128)S(1)}, f32[2,64,32]{2,1,0:T(8,128)S(1)}, u32[]{:S(2)}, u32[]{:S(2)}) %collective-permute-start.2) | collective-permute-done | bytes 16416 | tf_op jit(solution)/shard_map/ppermute | solution.py:293
  96.7 4.3 %multiply_reduce_fusion = f32[1024]{0:T(1024)S(1)} fusion(f32[2048]{0:T(1024)S(1)} %broadcast_subtract_fusion, bf16[32,2048]{1,0:T(8,128)(2,1)S(1)} %copy-done.2, f32[32]{0:T(128)S(1)} %broadcast_multiply_fusion.1, bf16[8,4,8,128]{3,2,1,0:T(8,128)(2,1)S(1)} %convert_bitcast_fusion), kind=kOutput, calls=%fused_computation.29 | convolution fusion | flops 811727872 | bytes 209024 | tf_op jit(solution)/shard_map/dot_general | solution.py:425
  101.0 2.5 %bitcast_reduce_fusion = (f32[1024,8]{0,1:T(8,128)S(1)}, f32[1024,1024]{0,1:T(8,128)S(1)}) fusion(f32[1024]{0:T(1024)S(1)} %bitcast.142, f32[1024]{0:T(1024)S(1)} %bitcast.144, f32[1024]{0:T(1024)S(1)} %add_rsqrt_fusion.3, f32[40,3072]{1,0:T(8,128)S(1)} %reshape.241, bf16[8,4,8,128]{3,2,1,0:T(8,128)(2,1)S(1)} %convert_bitcast_fusion), kind=kOutput, calls=%fused_computation.33 | convolution fusion | flops 407887872 | bytes 4435968 | tf_op jit(solution)/shard_map/dot_general | solution.py:434
  103.6 3.5 %add_convert_fusion = bf16[1024,1024]{0,1:T(8,128)(2,1)} fusion(f32[1024]{0:T(1024)S(1)} %bitcast.150, f32[1024]{0:T(1024)S(1)} %bitcast.149, f32[1024]{0:T(1024)S(1)} %add_rsqrt_fusion.3, f32[40,3072]{1,0:T(8,128)S(1)} %reshape.241, bf16[8,4,8,128]{3,2,1,0:T(8,128)(2,1)S(1)} %convert_bitcast_fusion), kind=kOutput, calls=%fused_computation.34 | convolution fusion | flops 406847488 | bytes 2306048 | tf_op jit(solution)/shard_map/dot_general | solution.py:434
  109.2 1.7 fusion.34
  110.9 62.1 %while.11 = (s32[]{:T(128)}, bf16[8,256,128]{1,2,0:T(8,128)(2,1)}, s32[8]{0:T(128)S(1)}, bf16[256,1024]{1,0:T(8,128)(2,1)}, bf16[1024,1024]{0,1:T(8,128)(2,1)S(1...) while((s32[]{:T(128)}, bf16[8,256,128]{1,2,0:T(8,128)(2,1)}, ...), condition=%wide.region_13.14_spmd.clone, body=%wide.region_10.13_spmd.clone.sunk | while | flops 170786816 | bytes 4013799 | solution.py:352
  114.0 1.5 fusion.92
  121.8 1.5 fusion.92
  129.6 1.5 fusion.92
  137.3 1.5 fusion.92
  145.1 1.5 fusion.92
  152.8 1.5 fusion.92
  160.6 1.5 fusion.92
  168.4 1.5 fusion.92
  173.0 3.7 %convolution_multiply_fusion.2 = f32[256,2048]{1,0:T(8,128)S(1)} fusion(bf16[256,1024]{0,1:T(8,128)(2,1)} %bitcast.151, bf16[2048,1024]{1,0:T(8,128)(2,1)} %bitcast.123, f32[2048]{0:T(1024)S(1)} %bitcast.148), kind=kOutput, calls=%fused_computation.37 | convolution fusion | flops 1074266112 | bytes 6823936 | tf_op jit(solution)/shard_map/dot_general | solution.py:485
  176.7 1.4 fusion.27
  (197 shorter events, 65.0 us)
Async XLA Ops:
  0.6 5.1 %copy-start = (bf16[2048,32]{0,1:T(8,128)(2,1)S(1)}, bf16[2048,32]{0,1:T(8,128)(2,1)}, u32[]{:S(2)}) copy-start(bf16[2048,32]{0,1:T(8,128)(2,1)} %param.23) | copy-start | bytes 393220
  0.6 8.8 %copy-start.6 = (bf16[256,1024]{1,0:T(8,128)(2,1)S(1)}, bf16[256,1024]{1,0:T(8,128)(2,1)}, u32[]{:S(2)}) copy-start(bf16[256,1024]{1,0:T(8,128)(2,1)} %param.36) | copy-start | bytes 1572868
  6.1 57.6 %collective-permute-start = (f32[2,2048]{1,0:T(2,128)S(1)}, f32[2,2048]{1,0:T(2,128)S(1)}, u32[]{:S(2)}, u32[]{:S(2)}) collective-permute-start(f32[2,2048]{1,0:T(2,128)S(1)} %reshape.236), channel_id=1, source_target_pairs={{0,128},{128,0},{1,129},{129,1},{2,130},{130,2},{3,131},{131,3},{4... | collective-permute-start | bytes 49160 | tf_op jit(solution)/shard_map/ppermute | solution.py:282
  9.6 1.3 copy-start.15
  9.6 1.5 copy-start.3
  9.6 2.1 %copy-start.2 = (bf16[32,2048]{1,0:T(8,128)(2,1)S(1)}, bf16[32,2048]{1,0:T(8,128)(2,1)}, u32[]{:S(2)}) copy-start(bf16[32,2048]{1,0:T(8,128)(2,1)} %embed_ref.1) | copy-start | bytes 393220
  9.7 2.2 %copy-start.4 = (f32[3,2048]{1,0:T(4,128)S(1)}, f32[3,2048]{1,0:T(4,128)}, u32[]{:S(2)}) copy-start(f32[3,2048]{1,0:T(4,128)} %modulation_ref.1) | copy-start | bytes 73732
  9.7 2.2 %copy-start.5 = (bf16[8,3072]{1,0:T(8,128)(2,1)S(1)}, bf16[8,3072]{1,0:T(8,128)(2,1)}, u32[]{:S(2)}) copy-start(bf16[8,3072]{1,0:T(8,128)(2,1)} %weight_ref.1) | copy-start | bytes 147460
  10.9 50.8 %copy-start.16 = (f32[4096]{0:T(1024)S(1)}, f32[4096]{0:T(1024)}, u32[]{:S(2)}) copy-start(f32[4096]{0:T(1024)} %param.27) | copy-start | bytes 49156
  10.9 52.7 %copy-start.17 = (f32[2,2048]{1,0:T(2,128)S(1)}, f32[2,2048]{1,0:T(2,128)}, u32[]{:S(2)}) copy-start(f32[2,2048]{1,0:T(2,128)} %param.24) | copy-start | bytes 49156
  58.6 1.9 %copy-start.1 = (bf16[2,2,4,8,2,16,512]{6,5,4,3,2,1,0:T(8,128)(2,1)}, bf16[2,2,4,8,2,16,512]{6,5,4,3,2,1,0:T(8,128)(2,1)S(1)}, u32[]{:S(2)}) copy-start(bf16[2,2,4,8,2,16,512]{6,5,4,3,2,1,0:T(8,128)(2,1)S(1)} %get-tuple-element.59) | copy-start | bytes 12582916
  61.0 40.0 %copy-start.12 = (f32[1,1024]{1,0:T(1,128)}, f32[1,1024]{1,0:T(1,128)S(1)}, u32[]{:S(2)}) copy-start(f32[1,1024]{1,0:T(1,128)S(1)} %get-tuple-element.201) | copy-start | bytes 12292
  65.1 19.8 %collective-permute-start.1 = (f32[2,64,32]{2,1,0:T(8,128)S(1)}, f32[2,64,32]{2,1,0:T(8,128)S(1)}, u32[]{:S(2)}, u32[]{:S(2)}) collective-permute-start(f32[2,64,32]{2,1,0:T(8,128)S(1)} %reshape.237), channel_id=1, source_target_pairs={{0,1},{1,2},{2,3},{3,4},{4,5},{5,6},{6,7},{7,8},{8,9},{9,10},{10,1... | collective-permute-start | bytes 49160 | tf_op jit(solution)/shard_map/ppermute | solution.py:290
  82.3 7.1 %collective-permute-start.2 = (f32[2,64,32]{2,1,0:T(8,128)S(1)}, f32[2,64,32]{2,1,0:T(8,128)S(1)}, u32[]{:S(2)}, u32[]{:S(2)}) collective-permute-start(f32[2,64,32]{2,1,0:T(8,128)S(1)} %reshape.237), channel_id=1, source_target_pairs={{1,0},{2,1},{3,2},{4,3},{5,4},{6,5},{7,6},{8,7},{9,8},{10,9},{11,1... | collective-permute-start | bytes 49160 | tf_op jit(solution)/shard_map/ppermute | solution.py:293
  90.4 1.1 copy-start.11
  90.4 1.1 copy-start.20
  93.3 2.0 %copy-start.9 = (bf16[2,1,128,32]{2,0,3,1:T(2,128)(2,1)}, bf16[2,1,128,32]{2,0,3,1:T(2,128)(2,1)S(1)}, u32[]{:S(2)}) copy-start(bf16[2,1,128,32]{2,0,3,1:T(2,128)(2,1)S(1)} %copy.158) | copy-start | bytes 49156
  103.5 3.5 %copy-start.13 = (f32[1,1024]{1,0:T(1,128)S(1)}, f32[1,1024]{1,0:T(1,128)}, u32[]{:S(2)}) copy-start(f32[1,1024]{1,0:T(1,128)} %copy-done.12) | copy-start | bytes 12292
  107.1 1.4 copy-start.8
  109.2 1.7 copy-start.19
  109.2 1.7 copy-start.23
  109.2 1.7 copy-start.24
  110.9 62.1 %copy-start.18 = (f32[1,2048]{1,0:T(1,128)S(1)}, f32[1,2048]{1,0:T(1,128)}, u32[]{:S(2)}) copy-start(f32[1,2048]{1,0:T(1,128)} %slice.120) | copy-start | bytes 24580
  173.0 3.7 %copy-start.10 = (bf16[2,1,128,32]{2,0,3,1:T(2,128)(2,1)S(1)}, bf16[2,1,128,32]{2,0,3,1:T(2,128)(2,1)}, u32[]{:S(2)}) copy-start(bf16[2,1,128,32]{2,0,3,1:T(2,128)(2,1)} %copy-done.9) | copy-start | bytes 49156
  (4 other events, 3.5 us)

commit v3 on v2

v3 whole, which is shorter than its diff:
```python
import jax
import jax.numpy as jnp
from jax import lax
from jax.experimental import pallas as pl
from jax.experimental.pallas import tpu as pltpu
from jax.sharding import PartitionSpec as P

HEADS = 8
STEPS = 50
MESH = pl.DeviceIdType.MESH
LOG2E = 1.4426950408889634

epsilon = 1e-06
flow_shift = 5.0
highest = lax.Precision.HIGHEST
f32 = jnp.float32
bf16 = jnp.bfloat16

def remote(src, dst, send_sem, recv_sem, device):
    return pltpu.make_async_remote_copy(
        src_ref=src, dst_ref=dst, send_sem=send_sem, recv_sem=recv_sem,
        device_id=device, device_id_type=MESH,
    )


class Place:
    def __init__(self):
        self.x_lo = lax.axis_index("cfg")
        seq = lax.axis_index("seq")
        self.seq = seq
        self.core = lax.rem(seq, 2)
        self.x_hi = lax.rem(lax.div(seq, 2), 2)
        self.z = lax.rem(lax.div(seq, 4), 8)
        self.y = lax.div(seq, 32)
        self.x = self.x_hi * 2 + self.x_lo
        self.member = self.x_lo * 4 + self.x_hi * 2 + self.core
        self.line = lax.div(seq, 4)

    def at(self, x=None, y=None, z=None, core=None):
        x = self.x if x is None else x
        y = self.y if y is None else y
        z = self.z if z is None else z
        core = self.core if core is None else core
        return (lax.rem(x, 2), ((y * 8 + z) * 2 + lax.div(x, 2)) * 2 + core)

    def member_device(self, member):
        return (lax.div(member, 4), self.line * 4 + lax.rem(member, 4))


def greet(place):
    barrier = pltpu.get_barrier_semaphore()
    partners = [place.member_device(lax.rem(place.member + d, 8)) for d in range(1, 8)]
    partners += [place.at(y=lax.rem(place.y + d, 4)) for d in range(1, 4)]
    partners += [place.at(z=lax.rem(place.z + d, 8)) for d in range(1, 8)]
    for other in (lax.rem(place.seq + 1, 128), lax.rem(place.seq + 127, 128)):
        partners += [(place.x_lo, other), (1 - place.x_lo, other)]
    for partner in partners:
        pl.semaphore_signal(barrier, inc=1, device_id=partner, device_id_type=MESH)
    return barrier, len(partners)

def layer_norm(values):
    centred = values - jnp.mean(values, -1, keepdims=True)
    return centred * lax.rsqrt(jnp.mean(centred * centred, -1, keepdims=True) + epsilon)


def sigma_at(step_value):
    fraction = 1.0 - step_value / STEPS
    return flow_shift * fraction / (1.0 + (flow_shift - 1.0) * fraction)


def split_two(values):
    high = values.astype(bf16).astype(f32)
    return high, values - high


def dot_nt(a, b):
    return lax.dot_general(a, b, (((1,), (1,)), ((), ())), preferred_element_type=f32)


def dot_nn(a, b):
    return jnp.dot(a, b, preferred_element_type=f32)


TAPS = (((0,), (1, 2), ()), ((), (0, 1), (2,)))


def coarse_weights(up_ref, offset):
    eye = (
        lax.broadcasted_iota(jnp.int32, (32, 32), 0) == lax.broadcasted_iota(jnp.int32, (32, 32), 1)
    ).astype(f32)
    bands = []
    for column in range(3):
        blocks = []
        for a in range(2):
            for c in range(2):
                block = eye if offset == 1 and column == 1 else jnp.zeros((32, 32), f32)
                for r in TAPS[a][offset]:
                    for k in TAPS[c][column]:
                        tap = (3 * r + k) * 32
                        block = block + up_ref[tap : tap + 32, :]
                blocks.append(block)
        bands.append(jnp.concatenate(blocks, 1))
    return jnp.concatenate(bands, 0)


def kernel(
    step_ref, guide_ref, length_ref,
    hidden_ref, coarse_mod_ref, final_ref, latent_ref, scales_ref, up_ref, up_bias_ref,
    embed_ref, bias_ref, modulation_ref, weight_ref, query_gain_ref, key_gain_ref,
    text_keys_ref, text_values_ref, output_ref,
    guided_out, fine_out, hidden_out,
    left, own_rows, group_rows, partial, z_parts, y_parts, folded,
    out_chunk, out_sibling, out_rows,
    velocity, latents, cells, grid_cells, pairs, query_tokens, key_tokens,
    centred_right, state_right, folded_right, shift_row,
    query_buf, key_buf, value_buf, text_key_buf, text_value_buf, ones_buf, attended,
    *sems,
):
    (
        a_send, a_recv, rz_send, rz_recv, ry_send, ry_recv, gz_send, gz_recv, gx_send, gx_recv,
        s_send, s_recv, wz_send, wz_recv, wp_send, wp_recv, wq_send, wq_recv, ws_send, ws_recv,
        v_send, v_recv, l_send, l_recv,
    ) = sems
    place = Place()
    core, z, y, member, seq, branch = (
        place.core, place.z, place.y, place.member, place.seq, place.x_lo
    )
    group_rows[...] = jnp.zeros_like(group_rows)
    barrier, count = greet(place)
    for part in range(8):
        own_rows[part] = weight_ref[:, part * 384 : (part + 1) * 384].astype(f32)
    eye = (
        lax.broadcasted_iota(jnp.int32, (8, 8), 0) == lax.broadcasted_iota(jnp.int32, (8, 8), 1)
    ).astype(bf16)
    turned = dot_nt(eye, output_ref[...])
    out_chunk[0] = turned[:, :512]
    out_chunk[1] = turned[:, 512:]
    for m in range(32):
        latents[1, m : m + 1, :] = latent_ref[m // 16 : m // 16 + 1, m % 16 * 128 : m % 16 * 128 + 128]
    pl.semaphore_wait(barrier, count)
    sibling = place.at(core=1 - core)
    swap = remote(out_chunk.at[1 - core], out_sibling, s_send, s_recv, sibling)
    swap.start()
    quarter = lax.rem(place.line, 4)
    spread = []
    for d in range(1, 8):
        target = lax.rem(member + d, 8)
        copy = remote(
            own_rows.at[target],
            group_rows.at[place.x_lo, quarter, place.x_hi * 2 + core],
            a_send.at[d], a_recv.at[d], place.member_device(target),
        )
        copy.start()
        spread.append(copy)
    after, before = lax.rem(seq + 1, 128), lax.rem(seq + 127, 128)
    latent_copies = [
        remote(latents.at[1], latents.at[0], l_send.at[0], l_recv.at[0], (branch, after)),
        remote(latents.at[1], latents.at[2], l_send.at[1], l_recv.at[1], (branch, before)),
    ]
    for copy in latent_copies:
        copy.start()
    group_rows[place.x_lo, quarter, place.x_hi * 2 + core] = own_rows[member]

    embed = embed_ref[...].astype(f32)
    scale = 1.0 + modulation_ref[1:2, :]
    embed_centred = embed - jnp.mean(embed, -1, keepdims=True)
    bias = bias_ref[...]
    bias_centred = bias - jnp.mean(bias, -1, keepdims=True)
    width = embed.shape[1]
    left[0:32] = embed_centred * scale
    left[32:40] = jnp.concatenate(
        [bias_centred * scale, modulation_ref[0:1, :], jnp.zeros((6, width), f32)], 0
    )

    swap.wait()
    mine, other = out_chunk[core], out_sibling[...]
    first = core == 0
    out_rows[core, place.x_lo, y, z, place.x_hi] = jnp.concatenate(
        [jnp.where(first, mine, other), jnp.where(first, other, mine)], 0
    ).astype(bf16)
    along_z = []
    for d in range(1, 8):
        slot = out_rows.at[core, place.x_lo, y, z, place.x_hi]
        copy = remote(slot, slot, wz_send.at[d], wz_recv.at[d], place.at(z=lax.rem(z + d, 8)))
        copy.start()
        along_z.append(copy)

    for copy in spread:
        copy.wait()
    column = pl.multiple_of(lax.div(place.line, 4) * 128, 128)
    total = jnp.dot(
        left[:, pl.ds(column, 128)], group_rows[0].reshape(128, 384), precision=highest
    ) + jnp.dot(
        left[:, pl.ds(1024 + column, 128)], group_rows[1].reshape(128, 384), precision=highest
    )
    for row in range(5):
        for block in range(3):
            partial[row * 3 + block] = total[
                row * 8 : row * 8 + 8, block * 128 : block * 128 + 128
            ]
    partial[15] = jnp.zeros((8, 128), f32)
    scatter = []
    for d in range(1, 8):
        target = lax.rem(z + d, 8)
        copy = remote(
            partial.at[pl.ds(target * 2, 2)], z_parts.at[z],
            rz_send.at[d], rz_recv.at[d], place.at(z=target),
        )
        copy.start()
        scatter.append(copy)
    z_parts[z] = partial[pl.ds(z * 2, 2)]

    for row in range(2):
        modulated = (
            layer_norm(hidden_ref[row * 64 : row * 64 + 64, :].astype(f32))
            * (1.0 + coarse_mod_ref[1:2, :])
            + coarse_mod_ref[0:1, :]
        ).astype(bf16)
        cells[row * 64 : row * 64 + 64, :] = dot_nn(modulated, final_ref[...])
    velocity[branch, 1] = jnp.concatenate(
        [cells[pl.ds(c, 32, stride=4), :] for c in range(4)], 1
    )
    velocity_copies = []
    targets = [
        ((1 - branch, seq), 1), ((branch, after), 0), ((1 - branch, after), 0),
        ((branch, before), 2), ((1 - branch, before), 2),
    ]
    for d, (target, slot) in enumerate(targets):
        copy = remote(
            velocity.at[branch, 1], velocity.at[branch, slot], v_send.at[d], v_recv.at[d], target
        )
        copy.start()
        velocity_copies.append(copy)

    for copy in along_z:
        copy.wait()
    first_at = y * (1 - core) + place.x * core
    second_at = place.x * (1 - core) + y * core

    def piece(p, q):
        px, py = q * (1 - core) + p * core, p * (1 - core) + q * core
        return out_rows.at[core, lax.rem(px, 2), py, :, lax.div(px, 2)]

    def piece_device(p, q):
        return place.at(x=q * (1 - core) + p * core, y=p * (1 - core) + q * core)

    along_p = []
    for d in range(1, 4):
        slot = piece(first_at, second_at)
        copy = remote(
            slot, slot, wp_send.at[d], wp_recv.at[d],
            piece_device(lax.rem(first_at + d, 4), second_at),
        )
        copy.start()
        along_p.append(copy)
    along_q = []

    def send_q(e):
        for d in range(1, 4):
            slot = piece(lax.rem(first_at + 4 - e, 4), second_at)
            copy = remote(
                slot, slot, wq_send.at[e, d], wq_recv.at[e, d],
                piece_device(first_at, lax.rem(second_at + d, 4)),
            )
            copy.start()
            along_q.append(copy)

    to_sibling = []

    def send_sibling(e, d):
        slot = piece(lax.rem(first_at + 4 - e, 4), lax.rem(second_at + 4 - d, 4))
        copy = remote(slot, slot, ws_send.at[e, d], ws_recv.at[e, d], sibling)
        copy.start()
        to_sibling.append(copy)

    send_q(0)
    send_sibling(0, 0)

    for copy in scatter:
        copy.wait()
    y_parts[y] = jnp.sum(z_parts[...], 0)
    over_y = []
    for d in range(1, 4):
        copy = remote(
            y_parts.at[y], y_parts.at[y], ry_send.at[d], ry_recv.at[d],
            place.at(y=lax.rem(y + d, 4)),
        )
        copy.start()
        over_y.append(copy)

    lane_zeros = jnp.zeros((61, width), f32)
    high, low = split_two(embed_centred)
    bias_high, bias_low = split_two(bias_centred)
    centred_right[...] = jnp.concatenate(
        [high, low, bias_high, bias_low, jnp.zeros((1, width), f32), lane_zeros], 0
    ).astype(bf16)
    bias_high, bias_rest = split_two(bias)
    bias_middle, bias_low = split_two(bias_rest)
    state_right[...] = jnp.concatenate(
        [embed, jnp.zeros((32, width), f32), bias_high, bias_middle, bias_low, lane_zeros], 0
    ).astype(bf16)
    same_head = (
        lax.div(lax.broadcasted_iota(jnp.int32, (256, 256), 0), 128)
        == lax.div(lax.broadcasted_iota(jnp.int32, (256, 256), 1), 128)
    ).astype(bf16)
    key_gain = jnp.concatenate([key_gain_ref[...]] * 2, 1)
    query_gain = jnp.concatenate([query_gain_ref[...]] * 2, 1) * (LOG2E * 128 ** (-0.5))

    def head_norm(values, gain):
        squares = dot_nn((values * values).astype(bf16), same_head)
        return (values * lax.rsqrt(squares * (1.0 / 128) + epsilon) * gain).astype(bf16)

    for pair in range(4):
        cols = slice(pair * 256, pair * 256 + 256)
        text_key_buf[:, cols] = head_norm(text_keys_ref[:, cols].astype(f32), key_gain)
    length = length_ref[0]
    real = lax.broadcasted_iota(jnp.int32, (256, 1), 0) < length
    text_value_buf[...] = jnp.where(real, text_values_ref[...].astype(f32), 0.0).astype(bf16)
    row_ok = [jnp.where(seq > 0, 1.0, 0.0), 1.0, 1.0, jnp.where(seq < 127, 1.0, 0.0)]
    for row in range(4):
        ones_buf[row * 256 : row * 256 + 256, :] = (
            jnp.ones((256, 128), f32) * row_ok[row]
        ).astype(bf16)
    ones_buf[1024:1280, :] = jnp.where(real, jnp.ones((256, 128), f32), 0.0).astype(bf16)

    for copy in over_y:
        copy.wait()
    folded[member, pl.ds(z * 2, 2)] = jnp.sum(y_parts[...], 0)
    gather_z = []
    for d in range(1, 8):
        slot = folded.at[member, pl.ds(z * 2, 2)]
        copy = remote(slot, slot, gz_send.at[d], gz_recv.at[d], place.at(z=lax.rem(z + d, 8)))
        copy.start()
        gather_z.append(copy)

    for copy in latent_copies + velocity_copies:
        copy.wait()
    slots = (
        lax.broadcasted_iota(jnp.int32, (32, 128), 0) * 128
        + lax.broadcasted_iota(jnp.int32, (32, 128), 1)
    )
    guidance = jnp.sum(
        jnp.where(slots == guide_ref[0], scales_ref[...], 0.0), axis=(0, 1), keepdims=True
    )
    step = jnp.full((1, 128), step_ref[0], jnp.int32)
    sigma_step = sigma_at((step + 1).astype(f32)) - sigma_at(step.astype(f32))
    for block in range(3):
        conditional, unconditional = velocity[0, block], velocity[1, block]
        guided = unconditional + guidance * (conditional - unconditional)
        if block == 1:
            for m in range(32):
                guided_out[m // 16 : m // 16 + 1, m % 16 * 128 : m % 16 * 128 + 128] = guided[
                    m : m + 1, :
                ]
        stepped = latents[block] + sigma_step * guided
        if block == 0:
            stepped = jnp.where(seq > 0, stepped, 0.0)
        if block == 2:
            stepped = jnp.where(seq < 127, stepped, 0.0)
        for c in range(4):
            grid_cells[pl.ds(8 + block * 128 + c, 32, stride=4), :] = stepped[
                :, c * 32 : c * 32 + 32
            ]
    grid_cells[0:8, :] = jnp.zeros((8, 32), f32)
    grid_cells[392:400, :] = jnp.zeros((8, 32), f32)
    cell = lax.rem(lax.broadcasted_iota(jnp.int32, (384, 32), 0), 64)
    around = jnp.concatenate(
        [
            jnp.where(cell == 0, 0.0, grid_cells[7:391, :]),
            grid_cells[8:392, :],
            jnp.where(cell == 63, 0.0, grid_cells[9:393, :]),
        ],
        1,
    )
    fine = jnp.concatenate([up_bias_ref[...]] * 4, 1)
    for offset in range(3):
        fine = fine + jnp.dot(
            around[offset * 64 : offset * 64 + 256],
            coarse_weights(up_ref, offset),
            precision=highest,
            preferred_element_type=f32,
        )
    own = fine[64:192]
    pairs[...] = jnp.where(branch == 0, own[:, :64], own[:, 64:])
    flat = jnp.concatenate([pairs[pl.ds(0, 64, stride=2), :], pairs[pl.ds(1, 64, stride=2), :]], 1)
    for m in range(64):
        fine_out[m // 32 : m // 32 + 1, m % 32 * 128 : m % 32 * 128 + 128] = flat[m : m + 1, :]

    lane = lax.broadcasted_iota(jnp.int32, (256, 128), 1)
    turns = [fine] + [pltpu.roll(fine, 32 * turn, axis=1) for turn in range(1, 4)]
    tail = jnp.where(lane < 67, 1.0, 0.0)
    groups = [
        jnp.where(lane < 32, turns[(4 - g) % 4], jnp.where(lane < 64, turns[(5 - g) % 4], tail))
        for g in range(4)
    ]
    for g in range(4):
        for row in range(4):
            start = row * 256 + g * 64
            key_tokens[start : start + 64, :] = groups[g][row * 64 : row * 64 + 64].astype(bf16)
    for c in range(2):
        chosen = jnp.where(branch == 0, groups[c], groups[2 + c])
        for row in range(2):
            query_tokens[pl.ds(row * 128 + c, 64, stride=2), :] = chosen[
                64 + row * 64 : 128 + row * 64
            ]
    own_tokens = query_tokens[...].astype(bf16)

    for e in range(1, 4):
        along_p[e - 1].wait()
        send_q(e)
        send_sibling(e, 0)
    for copy in gather_z:
        copy.wait()
    gather_x = []
    for d in range(1, 8):
        slot = folded.at[member]
        copy = remote(
            slot, slot, gx_send.at[d], gx_recv.at[d],
            place.member_device(lax.rem(member + d, 8)),
        )
        copy.start()
        gather_x.append(copy)

    def rstd_of(tokens):
        centred = dot_nn(tokens, centred_right[...])
        return lax.rsqrt(jnp.mean(centred * centred, -1, keepdims=True) + epsilon)

    query_rstd = rstd_of(own_tokens)
    key_rstd = [rstd_of(key_tokens[row * 256 : row * 256 + 256, :]) for row in range(4)]

    for copy in gather_x:
        copy.wait()
    for part in range(8):
        for block in range(3):
            rows = jnp.concatenate([folded[part, k * 3 + block] for k in range(4)], 0)
            rest = folded[part, 12 + block]
            high, low = split_two(rows)
            rest_high, rest_low = split_two(rest[0:1])
            at = part * 384 + block * 128
            folded_right[:, at : at + 128] = jnp.concatenate(
                [high, low, rest_high, rest_low, jnp.zeros((62, 128), f32)], 0
            ).astype(bf16)
            shift_row[:, at : at + 128] = rest[1:2]

    def project(tokens, rstd, start):
        cols = slice(start, start + 256)
        return rstd * dot_nn(tokens, folded_right[:, cols]) + shift_row[:, cols]

    for pair in range(4):
        cols = slice(pair * 256, pair * 256 + 256)
        query_buf[:, cols] = head_norm(project(own_tokens, query_rstd, pair * 256), query_gain)
    for row in range(4):
        rows = slice(row * 256, row * 256 + 256)
        tokens = key_tokens[rows, :]
        for pair in range(4):
            cols = slice(pair * 256, pair * 256 + 256)
            key_buf[rows, cols] = head_norm(
                project(tokens, key_rstd[row], 1024 + pair * 256), key_gain
            )
            value_buf[rows, cols] = (
                project(tokens, key_rstd[row], 2048 + pair * 256) * row_ok[row]
            ).astype(bf16)

    for head in range(HEADS):
        cols = slice(head * 128, head * 128 + 128)
        text_right = jnp.concatenate([text_value_buf[:, cols], ones_buf[1024:1280, :]], 1)
        for row in range(2):
            window = slice(row * 256, row * 256 + 768)
            query = query_buf[row * 128 : row * 128 + 128, cols]
            weights = jnp.exp2(dot_nt(query, key_buf[window, cols])).astype(bf16)
            text_weights = jnp.exp2(dot_nt(query, text_key_buf[:, cols])).astype(bf16)
            right = jnp.concatenate([value_buf[window, cols], ones_buf[window, :]], 1)
            sums = dot_nn(weights, right) + dot_nn(text_weights, text_right)
            attended[row * 128 : row * 128 + 128, cols] = (sums[:, :128] / sums[:, 128:]).astype(
                bf16
            )
        if head >= 2:
            for item in range((head - 2) * 2, (head - 2) * 2 + 2):
                along_q[item].wait()
                send_sibling(item // 3, item % 3 + 1)

    for copy in to_sibling:
        copy.wait()
    for block in range(8):
        cols = slice(block * 256, block * 256 + 256)
        total = dot_nn(own_tokens, state_right[:, cols])
        output = jnp.zeros((256, 256), f32)
        for half in range(2):
            rows = out_rows[half, block // 4, block % 4].reshape(256, 512)
            output = output + dot_nt(attended[:, half * 512 : half * 512 + 512], rows)
        hidden_out[:, cols] = (total + modulation_ref[2:3, cols] * output).astype(bf16)


def per_device(
    coarse_hidden,
    coarse_modulation,
    final_weight,
    coarse_latent,
    step_index,
    guide_index,
    guide_scales,
    upsample_weight,
    upsample_bias,
    embed_weight,
    embed_bias,
    fine_modulation,
    project_weight,
    query_gain,
    key_gain,
    text_keys,
    text_values,
    text_length,
    output_weight,
):
    dma = pltpu.SemaphoreType.DMA
    sems = []
    for shape in [(8,), (8,), (4,), (8,), (8,)]:
        sems += [dma(shape), dma(shape)]
    sems += [dma, dma]
    for shape in [(8,), (4,), (4, 4), (4, 4), (5,), (2,)]:
        sems += [dma(shape), dma(shape)]
    vmem = pl.BlockSpec(memory_space=pltpu.VMEM)
    smem = pl.BlockSpec(memory_space=pltpu.SMEM)
    guided, fine, hidden = pl.pallas_call(
        kernel,
        out_shape=(
            jax.ShapeDtypeStruct((2, 2048), f32),
            jax.ShapeDtypeStruct((2, 4096), f32),
            jax.ShapeDtypeStruct((256, 2048), bf16),
        ),
        in_specs=[smem] * 3 + [vmem] * 16,
        out_specs=(vmem, vmem, vmem),
        scratch_shapes=[
            pltpu.VMEM((40, 2048), f32),
            pltpu.VMEM((8, 8, 384), f32),
            pltpu.VMEM((2, 4, 4, 8, 384), f32),
            pltpu.VMEM((16, 8, 128), f32),
            pltpu.VMEM((8, 2, 8, 128), f32),
            pltpu.VMEM((4, 2, 8, 128), f32),
            pltpu.VMEM((8, 16, 8, 128), f32),
            pltpu.VMEM((2, 8, 512), f32),
            pltpu.VMEM((8, 512), f32),
            pltpu.VMEM((2, 2, 4, 8, 2, 16, 512), bf16),
            pltpu.VMEM((2, 3, 32, 128), f32),
            pltpu.VMEM((3, 32, 128), f32),
            pltpu.VMEM((128, 32), f32),
            pltpu.VMEM((400, 32), f32),
            pltpu.VMEM((128, 64), f32),
            pltpu.VMEM((256, 128), f32),
            pltpu.VMEM((1024, 128), bf16),
            pltpu.VMEM((128, 2048), bf16),
            pltpu.VMEM((128, 2048), bf16),
            pltpu.VMEM((128, 3072), bf16),
            pltpu.VMEM((1, 3072), f32),
            pltpu.VMEM((256, 1024), bf16),
            pltpu.VMEM((1024, 1024), bf16),
            pltpu.VMEM((1024, 1024), bf16),
            pltpu.VMEM((256, 1024), bf16),
            pltpu.VMEM((256, 1024), bf16),
            pltpu.VMEM((1280, 128), bf16),
            pltpu.VMEM((256, 1024), bf16),
        ]
        + sems,
        compiler_params=pltpu.CompilerParams(
            collective_id=0, has_side_effects=True, vmem_limit_bytes=48 * 1024 * 1024
        ),
    )(
        step_index,
        guide_index,
        text_length,
        coarse_hidden.reshape(128, 2048),
        coarse_modulation[0],
        final_weight,
        coarse_latent,
        guide_scales.reshape(32, 128),
        upsample_weight,
        upsample_bias[None],
        embed_weight,
        embed_bias[None],
        fine_modulation,
        project_weight,
        query_gain[None],
        key_gain[None],
        text_keys,
        text_values,
        output_weight,
    )
    return guided, fine.reshape(2, 1, 4096), hidden.reshape(2, 1, 128, 2048)


def solution(mesh):
    placed = (
        P("cfg", "seq", None, None),
        P("cfg", None, None),
        P(),
        P("seq", None),
        P(),
        P(),
        P(),
        P(),
        P(),
        P(),
        P(),
        P(),
        P(("cfg", "seq"), None),
        P(),
        P(),
        P(),
        P(),
        P(),
        P(None, ("cfg", "seq")),
    )
    return jax.shard_map(
        per_device,
        mesh=mesh,
        in_specs=placed,
        out_specs=(P("seq", None), P("seq", "cfg", None), P("seq", "cfg", None, None)),
        check_vma=False,
    )
```

time: 182 us -> 68.9 us (0.38); the launches traced: 178 us -> 68.5 us
  matrix products: 58.3 us -> 0 us
  local copies, waits for them, and re-layouts: 34.5 us -> 9.42 us
  other arithmetic: 18.3 us -> 0 us
  Pallas kernels: 46.7 us -> 56.3 us
  starting transfers between devices: 6.84 us -> 0 us
  loops' own time: 5.72 us -> 0 us
  waiting for transfers between devices: 4.42 us -> 0 us
    dot_general x41 -> x0, matrix products: 58.3 us -> none  [the longest x8 11.8 us: one_head(): lax.dot_general(query_part, key_part, dims, preferred_element_type=jnp.fl...]
    transpose x1 -> x0, local copies, waits for them, and re-layouts: 10.7 us -> none  [gather_parts(): output_rows = rows.transpose(1, 2, 3, 4, 5, 0, 6).reshape(2048, 1024)]
    pallas_call x1, Pallas kernels: 46.7 us -> 56.3 us  [per_device(): pl.pallas_call(kernel, out_shape=(jax.ShapeDtypeStruct((2, 2048), f32), j...]
    ppermute x3 -> x0, starting transfers between devices: 6.84 us -> none  [the longest x1 2.61 us: with_halo(): lax.ppermute(lax.slice_in_dim(block, 0, width, axis=dim), axis, backward)]
    dynamic_update_slice x16 -> x0, local copies, waits for them, and re-layouts: 5.97 us -> none  [attend(): stacked = lax.map(one_head, jnp.arange(heads, dtype=jnp.int32))]
    another operation x1 -> x0, loops' own time: 5.72 us -> none  [attend(): stacked = lax.map(one_head, jnp.arange(heads, dtype=jnp.int32))]
    lt x8 -> x0, other arithmetic: 5.36 us -> none  [per_device(): jnp.arange(text_keys.shape[0], dtype=jnp.int32) < text_length[0]]
    dynamic_slice x9 -> x0, local copies, waits for them, and re-layouts: 5.27 us -> none  [the longest x8 5.17 us: attend(): stacked = lax.map(one_head, jnp.arange(heads, dtype=jnp.int32))]
  transfers between devices with their start and end apart: 3 -> 0, of which waited for: 1 -> 0; matrix products, arithmetic and copies ran while one was open for 11% -> 0% of each run, Pallas kernels for 26% -> 0%
where the time goes in v3:
time: 68.9 us; the launch traced here: 68.5 us
  Pallas kernels  56.3 us (82%)
  local copies, waits for them, and re-layouts  9.42 us (14%)
  between operations  2.74 us (4%)
    pallas_call x1, Pallas kernels, per_device(): pl.pallas_call(kernel, out_shape=(jax.ShapeDtypeStruct((2, 2048), f32), j...  56.3 us
    unnamed x32, local copies, waits for them, and re-layouts  9.42 us

profile of v3, /device:TPU:1, one launch (start us, length us, event | category | flops | bytes accessed | tf_op | source)
XLA Modules:
  0.0 68.5 jit_solution(18290785560899062583)
XLA Ops:
  2.6 0.0 copy-start.9
  2.6 0.0 copy-start.10
  2.6 0.0 copy-start.11
  2.6 0.0 copy-start.12
  2.6 0.0 copy-start
  2.6 0.0 copy-start.1
  2.6 1.0 %copy.23.up_ref = f32[288,32]{1,0:T(8,128)S(1)} copy(f32[288,32]{0,1:T(8,128)} %param.26) | data formatting | bytes 73728 | tf_op args[7]
  3.6 0.9 %copy.24.output_ref = bf16[1024,8]{1,0:T(8,128)(2,1)S(1)} copy(bf16[1024,8]{0,1:T(8,128)(2,1)} %param.37) | data formatting | bytes 32768 | tf_op args[18]
  4.5 0.0 copy-start.4
  4.5 0.0 copy-start.5
  4.5 1.2 %copy.22.final_ref = bf16[2048,32]{1,0:T(8,128)(2,1)S(1)} copy(bf16[2048,32]{0,1:T(8,128)(2,1)} %param.21) | data formatting | bytes 262144 | tf_op args[2]
  5.7 0.0 copy-done.9
  5.8 0.0 copy-done.10
  5.8 0.0 copy-done.11
  5.8 0.0 copy-start.2
  5.8 1.0 %copy-done.2 = bf16[256,1024]{1,0:T(8,128)(2,1)S(1)} copy-done((bf16[256,1024]{1,0:T(8,128)(2,1)S(1)}, bf16[256,1024]{1,0:T(8,128)(2,1)}, u32[]{:S(2)}) %copy-start.2) | copy-done | bytes 524312
  6.9 0.9 %copy-done.3 = bf16[32,2048]{1,0:T(8,128)(2,1)S(1)} copy-done((bf16[32,2048]{1,0:T(8,128)(2,1)S(1)}, bf16[32,2048]{1,0:T(8,128)(2,1)}, u32[]{:S(2)}) %copy-start.3) | copy-done | bytes 131096
  7.8 0.7 %copy-done.6 = f32[1,2,2048]{2,1,0:T(2,128)S(1)} copy-done((f32[1,2,2048]{2,1,0:T(2,128)S(1)}, f32[1,2,2048]{2,1,0:T(2,128)}, u32[]{:S(2)}) %copy-start.6) | copy-done | bytes 16408
  8.5 0.7 %copy-done.7 = f32[2,2048]{1,0:T(2,128)S(1)} copy-done((f32[2,2048]{1,0:T(2,128)S(1)}, f32[2,2048]{1,0:T(2,128)}, u32[]{:S(2)}) %copy-start.7) | copy-done | bytes 16408
  9.2 0.7 %copy-done.8 = f32[4096]{0:T(1024)S(1)} copy-done((f32[4096]{0:T(1024)S(1)}, f32[4096]{0:T(1024)}, u32[]{:S(2)}) %copy-start.8) | copy-done | bytes 16408
  9.9 56.3 %shard_map.202 = (f32[2,2048]{1,0:T(2,128)S(1)}, f32[2,4096]{1,0:T(2,128)S(1)}, bf16[256,2048]{1,0:T(8,128)(2,1)S(1)}) custom-call(s32[1]{0:T(128)S(6)} %copy.29.step_ref, s32[1]{0:T(128)S(6)} %copy.30.guide_ref, s32[1]{0:T(128)S(6)} %copy.31.length_ref, bf16[128,2048]{1,0:T(8,128)(2,1)S(1)} %bitcast.12, f32[2,2048]{1,0:T(2,128)S(1)} %bitcast.14, ...), custom_call_target="tpu_custom_call" | custom-call | tf_op jit(solution)/shard_map/pallas_call | solution.py:524
  66.2 0.6 copy.25
  66.9 0.6 copy.32
  67.5 1.0 %copy.33 = bf16[2,1,128,2048]{3,2,1,0:T(8,128)(2,1)} copy(bf16[2,1,128,2048]{3,2,1,0:T(8,128)(2,1)S(1)} %bitcast.11) | data formatting | bytes 2097152
  (9 shorter events, 0.0 us)
Async XLA Ops:
  2.6 3.2 %copy-start.9 = (f32[2048]{0:T(1024)S(1)}, f32[2048]{0:T(1024)}, u32[]{:S(2)}) copy-start(f32[2048]{0:T(1024)} %param.29) | copy-start | bytes 24580
  2.6 3.2 %copy-start.10 = (f32[32]{0:T(128)S(1)}, f32[32]{0:T(128)}, u32[]{:S(2)}) copy-start(f32[32]{0:T(128)} %param.27) | copy-start | bytes 388
  2.6 3.2 %copy-start.11 = (f32[128]{0:T(128)S(1)}, f32[128]{0:T(128)}, u32[]{:S(2)}) copy-start(f32[128]{0:T(128)} %param.32) | copy-start | bytes 1540
  2.6 3.2 %copy-start.12 = (f32[128]{0:T(128)S(1)}, f32[128]{0:T(128)}, u32[]{:S(2)}) copy-start(f32[128]{0:T(128)} %param.33) | copy-start | bytes 1540
  2.6 3.2 %copy-start = (bf16[1,2,64,2048]{3,2,1,0:T(8,128)(2,1)S(1)}, bf16[1,2,64,2048]{3,2,1,0:T(8,128)(2,1)}, u32[]{:S(2)}) copy-start(bf16[1,2,64,2048]{3,2,1,0:T(8,128)(2,1)} %param.19) | copy-start | bytes 1572868
  2.6 3.2 %copy-start.1 = (bf16[256,1024]{1,0:T(8,128)(2,1)S(1)}, bf16[256,1024]{1,0:T(8,128)(2,1)}, u32[]{:S(2)}) copy-start(bf16[256,1024]{1,0:T(8,128)(2,1)} %text_keys_ref.1) | copy-start | bytes 1572868
  4.5 1.3 %copy-start.4 = (bf16[8,3072]{1,0:T(8,128)(2,1)S(1)}, bf16[8,3072]{1,0:T(8,128)(2,1)}, u32[]{:S(2)}) copy-start(bf16[8,3072]{1,0:T(8,128)(2,1)} %weight_ref.1) | copy-start | bytes 147460
  4.5 1.3 %copy-start.5 = (f32[3,2048]{1,0:T(4,128)S(1)}, f32[3,2048]{1,0:T(4,128)}, u32[]{:S(2)}) copy-start(f32[3,2048]{1,0:T(4,128)} %modulation_ref.1) | copy-start | bytes 73732
  5.8 1.0 %copy-start.2 = (bf16[256,1024]{1,0:T(8,128)(2,1)S(1)}, bf16[256,1024]{1,0:T(8,128)(2,1)}, u32[]{:S(2)}) copy-start(bf16[256,1024]{1,0:T(8,128)(2,1)} %text_values_ref.1) | copy-start | bytes 1572868
  6.9 0.9 %copy-start.3 = (bf16[32,2048]{1,0:T(8,128)(2,1)S(1)}, bf16[32,2048]{1,0:T(8,128)(2,1)}, u32[]{:S(2)}) copy-start(bf16[32,2048]{1,0:T(8,128)(2,1)} %embed_ref.1) | copy-start | bytes 393220
  7.8 0.7 %copy-start.6 = (f32[1,2,2048]{2,1,0:T(2,128)S(1)}, f32[1,2,2048]{2,1,0:T(2,128)}, u32[]{:S(2)}) copy-start(f32[1,2,2048]{2,1,0:T(2,128)} %param.20) | copy-start | bytes 49156
  8.5 0.7 %copy-start.7 = (f32[2,2048]{1,0:T(2,128)S(1)}, f32[2,2048]{1,0:T(2,128)}, u32[]{:S(2)}) copy-start(f32[2,2048]{1,0:T(2,128)} %latent_ref.1) | copy-start | bytes 49156
  9.2 0.7 %copy-start.8 = (f32[4096]{0:T(1024)S(1)}, f32[4096]{0:T(1024)}, u32[]{:S(2)}) copy-start(f32[4096]{0:T(1024)} %param.25) | copy-start | bytes 49156

commit v4 on v3

--- a/solution.py
+++ b/solution.py
@@ -89,26 +89,43 @@
         lax.broadcasted_iota(jnp.int32, (32, 32), 0) == lax.broadcasted_iota(jnp.int32, (32, 32), 1)
     ).astype(f32)
     bands = []
-    for column in range(3):
-        blocks = []
-        for a in range(2):
-            for c in range(2):
+    for a in range(2):
+        for c in range(2):
+            blocks = []
+            for column in range(3):
                 block = eye if offset == 1 and column == 1 else jnp.zeros((32, 32), f32)
                 for r in TAPS[a][offset]:
                     for k in TAPS[c][column]:
                         tap = (3 * r + k) * 32
-                        block = block + up_ref[tap : tap + 32, :]
+                        block = block + up_ref[:, tap : tap + 32]
                 blocks.append(block)
-        bands.append(jnp.concatenate(blocks, 1))
+            bands.append(jnp.concatenate(blocks, 1))
     return jnp.concatenate(bands, 0)
 
 
 def kernel(
-    step_ref, guide_ref, length_ref,
-    hidden_ref, coarse_mod_ref, final_ref, latent_ref, scales_ref, up_ref, up_bias_ref,
-    embed_ref, bias_ref, modulation_ref, weight_ref, query_gain_ref, key_gain_ref,
-    text_keys_ref, text_values_ref, output_ref,
-    guided_out, fine_out, hidden_out,
+    step_ref, guide_ref, length_ref, weight_ref, output_ref, *refs
+):
+    stored, refs = refs[:14], refs[14:]
+    (guided_out, fine_out, hidden_out), held, refs = refs[:3], refs[3:17], refs[17:]
+    (
+        embed_ref, modulation_ref, bias_ref, latent_ref, hidden_ref, coarse_mod_ref, final_ref,
+        text_keys_ref, key_gain_ref, text_values_ref, scales_ref, up_ref, up_bias_ref,
+        query_gain_ref,
+    ) = held
+    run(
+        step_ref, guide_ref, length_ref, weight_ref, output_ref, stored, held,
+        embed_ref, modulation_ref, bias_ref, latent_ref, hidden_ref, coarse_mod_ref, final_ref,
+        text_keys_ref, key_gain_ref, text_values_ref, scales_ref, up_ref, up_bias_ref,
+        query_gain_ref, guided_out, fine_out, hidden_out, *refs
+    )
+
+
+def run(
+    step_ref, guide_ref, length_ref, weight_ref, output_ref, stored, held,
+    embed_ref, modulation_ref, bias_ref, latent_ref, hidden_ref, coarse_mod_ref, final_ref,
+    text_keys_ref, key_gain_ref, text_values_ref, scales_ref, up_ref, up_bias_ref,
+    query_gain_ref, guided_out, fine_out, hidden_out,
     left, own_rows, group_rows, partial, z_parts, y_parts, folded,
     out_chunk, out_sibling, out_rows,
     velocity, latents, cells, grid_cells, pairs, query_tokens, key_tokens,
@@ -119,8 +136,14 @@
     (
         a_send, a_recv, rz_send, rz_recv, ry_send, ry_recv, gz_send, gz_recv, gx_send, gx_recv,
         s_send, s_recv, wz_send, wz_recv, wp_send, wp_recv, wq_send, wq_recv, ws_send, ws_recv,
-        v_send, v_recv, l_send, l_recv,
+        v_send, v_recv, l_send, l_recv, load_sem,
     ) = sems
+    loads = [
+        pltpu.make_async_copy(source, target, load_sem.at[i])
+        for i, (source, target) in enumerate(zip(stored, held))
+    ]
+    for load in loads:
+        load.start()
     place = Place()
     core, z, y, member, seq, branch = (
         place.core, place.z, place.y, place.member, place.seq, place.x_lo
@@ -129,12 +152,11 @@
     barrier, count = greet(place)
     for part in range(8):
         own_rows[part] = weight_ref[:, part * 384 : (part + 1) * 384].astype(f32)
-    eye = (
-        lax.broadcasted_iota(jnp.int32, (8, 8), 0) == lax.broadcasted_iota(jnp.int32, (8, 8), 1)
-    ).astype(bf16)
-    turned = dot_nt(eye, output_ref[...])
+    turned = output_ref[...].astype(f32)
     out_chunk[0] = turned[:, :512]
     out_chunk[1] = turned[:, 512:]
+    for load in loads[:4]:
+        load.wait()
     for m in range(32):
         latents[1, m : m + 1, :] = latent_ref[m // 16 : m // 16 + 1, m % 16 * 128 : m % 16 * 128 + 128]
     pl.semaphore_wait(barrier, count)
@@ -172,6 +194,30 @@
         [bias_centred * scale, modulation_ref[0:1, :], jnp.zeros((6, width), f32)], 0
     )
 
+    for copy in spread:
+        copy.wait()
+    column = pl.multiple_of(lax.div(place.line, 4) * 128, 128)
+    total = jnp.dot(
+        left[:, pl.ds(column, 128)], group_rows[0].reshape(128, 384), precision=highest
+    ) + jnp.dot(
+        left[:, pl.ds(1024 + column, 128)], group_rows[1].reshape(128, 384), precision=highest
+    )
+    for row in range(5):
+        for block in range(3):
+            place_at = block * 4 + row if row < 4 else 12 + block
+            partial[place_at] = total[row * 8 : row * 8 + 8, block * 128 : block * 128 + 128]
+    partial[15] = jnp.zeros((8, 128), f32)
+    scatter = []
+    for d in range(1, 8):
+        target = lax.rem(z + d, 8)
+        copy = remote(
+            partial.at[pl.ds(target * 2, 2)], z_parts.at[z],
+            rz_send.at[d], rz_recv.at[d], place.at(z=target),
+        )
+        copy.start()
+        scatter.append(copy)
+    z_parts[z] = partial[pl.ds(z * 2, 2)]
+
     swap.wait()
     mine, other = out_chunk[core], out_sibling[...]
     first = core == 0
@@ -185,38 +231,15 @@
         copy.start()
         along_z.append(copy)
 
-    for copy in spread:
-        copy.wait()
-    column = pl.multiple_of(lax.div(place.line, 4) * 128, 128)
-    total = jnp.dot(
-        left[:, pl.ds(column, 128)], group_rows[0].reshape(128, 384), precision=highest
-    ) + jnp.dot(
-        left[:, pl.ds(1024 + column, 128)], group_rows[1].reshape(128, 384), precision=highest
-    )
-    for row in range(5):
-        for block in range(3):
-            partial[row * 3 + block] = total[
-                row * 8 : row * 8 + 8, block * 128 : block * 128 + 128
-            ]
-    partial[15] = jnp.zeros((8, 128), f32)
-    scatter = []
-    for d in range(1, 8):
-        target = lax.rem(z + d, 8)
-        copy = remote(
-            partial.at[pl.ds(target * 2, 2)], z_parts.at[z],
-            rz_send.at[d], rz_recv.at[d], place.at(z=target),
-        )
-        copy.start()
-        scatter.append(copy)
-    z_parts[z] = partial[pl.ds(z * 2, 2)]
-
+    for load in loads[4:7]:
+        load.wait()
     for row in range(2):
         modulated = (
             layer_norm(hidden_ref[row * 64 : row * 64 + 64, :].astype(f32))
             * (1.0 + coarse_mod_ref[1:2, :])
             + coarse_mod_ref[0:1, :]
         ).astype(bf16)
-        cells[row * 64 : row * 64 + 64, :] = dot_nn(modulated, final_ref[...])
+        cells[row * 64 : row * 64 + 64, :] = dot_nt(modulated, final_ref[...])
     velocity[branch, 1] = jnp.concatenate(
         [cells[pl.ds(c, 32, stride=4), :] for c in range(4)], 1
     )
@@ -232,6 +255,18 @@
         copy.start()
         velocity_copies.append(copy)
 
+    for copy in scatter:
+        copy.wait()
+    y_parts[y] = jnp.sum(z_parts[...], 0)
+    over_y = []
+    for d in range(1, 4):
+        copy = remote(
+            y_parts.at[y], y_parts.at[y], ry_send.at[d], ry_recv.at[d],
+            place.at(y=lax.rem(y + d, 4)),
+        )
+        copy.start()
+        over_y.append(copy)
+
     for copy in along_z:
         copy.wait()
     first_at = y * (1 - core) + place.x * core
@@ -276,17 +311,8 @@
     send_q(0)
     send_sibling(0, 0)
 
-    for copy in scatter:
-        copy.wait()
-    y_parts[y] = jnp.sum(z_parts[...], 0)
-    over_y = []
-    for d in range(1, 4):
-        copy = remote(
-            y_parts.at[y], y_parts.at[y], ry_send.at[d], ry_recv.at[d],
-            place.at(y=lax.rem(y + d, 4)),
-        )
-        copy.start()
-        over_y.append(copy)
+    for load in loads[7:]:
+        load.wait()
 
     lane_zeros = jnp.zeros((61, width), f32)
     high, low = split_two(embed_centred)
@@ -325,10 +351,13 @@
 
     for copy in over_y:
         copy.wait()
-    folded[member, pl.ds(z * 2, 2)] = jnp.sum(y_parts[...], 0)
+    summed = jnp.sum(y_parts[...], 0)
+    high, low = split_two(summed)
+    low = jnp.concatenate([jnp.zeros((2, 2, 128), f32), low[:, :6]], 1)
+    folded[member, z] = jnp.where(z >= 6, high + low, summed).reshape(16, 128).astype(bf16)
     gather_z = []
     for d in range(1, 8):
-        slot = folded.at[member, pl.ds(z * 2, 2)]
+        slot = folded.at[member, z]
         copy = remote(slot, slot, gz_send.at[d], gz_recv.at[d], place.at(z=lax.rem(z + d, 8)))
         copy.start()
         gather_z.append(copy)
@@ -374,9 +403,10 @@
     )
     fine = jnp.concatenate([up_bias_ref[...]] * 4, 1)
     for offset in range(3):
-        fine = fine + jnp.dot(
+        fine = fine + lax.dot_general(
             around[offset * 64 : offset * 64 + 256],
             coarse_weights(up_ref, offset),
+            (((1,), (1,)), ((), ())),
             precision=highest,
             preferred_element_type=f32,
         )
@@ -384,7 +414,7 @@
     pairs[...] = jnp.where(branch == 0, own[:, :64], own[:, 64:])
     flat = jnp.concatenate([pairs[pl.ds(0, 64, stride=2), :], pairs[pl.ds(1, 64, stride=2), :]], 1)
     for m in range(64):
-        fine_out[m // 32 : m // 32 + 1, m % 32 * 128 : m % 32 * 128 + 128] = flat[m : m + 1, :]
+        fine_out[m // 32, :, m % 32 * 128 : m % 32 * 128 + 128] = flat[m : m + 1, :]
 
     lane = lax.broadcasted_iota(jnp.int32, (256, 128), 1)
     turns = [fine] + [pltpu.roll(fine, 32 * turn, axis=1) for turn in range(1, 4)]
@@ -405,10 +435,6 @@
             ]
     own_tokens = query_tokens[...].astype(bf16)
 
-    for e in range(1, 4):
-        along_p[e - 1].wait()
-        send_q(e)
-        send_sibling(e, 0)
     for copy in gather_z:
         copy.wait()
     gather_x = []
@@ -421,6 +447,10 @@
         copy.start()
         gather_x.append(copy)
 
+    for e in range(1, 4):
+        along_p[e - 1].wait()
+        send_q(e)
+        send_sibling(e, 0)
     def rstd_of(tokens):
         centred = dot_nn(tokens, centred_right[...])
         return lax.rsqrt(jnp.mean(centred * centred, -1, keepdims=True) + epsilon)
@@ -432,15 +462,16 @@
         copy.wait()
     for part in range(8):
         for block in range(3):
-            rows = jnp.concatenate([folded[part, k * 3 + block] for k in range(4)], 0)
-            rest = folded[part, 12 + block]
-            high, low = split_two(rows)
-            rest_high, rest_low = split_two(rest[0:1])
             at = part * 384 + block * 128
-            folded_right[:, at : at + 128] = jnp.concatenate(
-                [high, low, rest_high, rest_low, jnp.zeros((62, 128), f32)], 0
+            folded_right[0:32, at : at + 128] = folded[part, block * 2 : block * 2 + 2].reshape(
+                32, 128
+            )
+            rest = folded[part, 6 + block // 2].astype(f32)[block % 2 * 8 : block % 2 * 8 + 8]
+            folded_right[32:80, at : at + 128] = jnp.concatenate(
+                [jnp.zeros((32, 128), f32), rest[0:1], rest[2:3], jnp.zeros((14, 128), f32)], 0
             ).astype(bf16)
-            shift_row[:, at : at + 128] = rest[1:2]
+            folded_right[80:128, at : at + 128] = jnp.zeros((48, 128), bf16)
+            shift_row[:, at : at + 128] = rest[1:2] + rest[3:4]
 
     def project(tokens, rstd, start):
         cols = slice(start, start + 256)
@@ -519,25 +550,34 @@
     sems += [dma, dma]
     for shape in [(8,), (4,), (4, 4), (4, 4), (5,), (2,)]:
         sems += [dma(shape), dma(shape)]
+    sems += [dma((14,))]
+    stored = [
+        embed_weight, fine_modulation, embed_bias[None], coarse_latent,
+        coarse_hidden.reshape(128, 2048), coarse_modulation[0], final_weight.T,
+        text_keys, key_gain[None], text_values, guide_scales.reshape(32, 128),
+        upsample_weight.T, upsample_bias[None], query_gain[None],
+    ]
+    hbm = pl.BlockSpec(memory_space=pltpu.HBM)
     vmem = pl.BlockSpec(memory_space=pltpu.VMEM)
     smem = pl.BlockSpec(memory_space=pltpu.SMEM)
     guided, fine, hidden = pl.pallas_call(
         kernel,
         out_shape=(
             jax.ShapeDtypeStruct((2, 2048), f32),
-            jax.ShapeDtypeStruct((2, 4096), f32),
+            jax.ShapeDtypeStruct((2, 1, 4096), f32),
             jax.ShapeDtypeStruct((256, 2048), bf16),
         ),
-        in_specs=[smem] * 3 + [vmem] * 16,
+        in_specs=[smem] * 3 + [vmem] * 2 + [hbm] * 14,
         out_specs=(vmem, vmem, vmem),
-        scratch_shapes=[
+        scratch_shapes=[pltpu.VMEM(array.shape, array.dtype) for array in stored]
+        + [
             pltpu.VMEM((40, 2048), f32),
             pltpu.VMEM((8, 8, 384), f32),
             pltpu.VMEM((2, 4, 4, 8, 384), f32),
             pltpu.VMEM((16, 8, 128), f32),
             pltpu.VMEM((8, 2, 8, 128), f32),
             pltpu.VMEM((4, 2, 8, 128), f32),
-            pltpu.VMEM((8, 16, 8, 128), f32),
+            pltpu.VMEM((8, 8, 16, 128), bf16),
             pltpu.VMEM((2, 8, 512), f32),
             pltpu.VMEM((8, 512), f32),
             pltpu.VMEM((2, 2, 4, 8, 2, 16, 512), bf16),
@@ -562,30 +602,12 @@
         ]
         + sems,
         compiler_params=pltpu.CompilerParams(
-            collective_id=0, has_side_effects=True, vmem_limit_bytes=48 * 1024 * 1024
+            collective_id=0, has_side_effects=True, vmem_limit_bytes=56 * 1024 * 1024
         ),
     )(
-        step_index,
-        guide_index,
-        text_length,
-        coarse_hidden.reshape(128, 2048),
-        coarse_modulation[0],
-        final_weight,
-        coarse_latent,
-        guide_scales.reshape(32, 128),
-        upsample_weight,
-        upsample_bias[None],
-        embed_weight,
-        embed_bias[None],
-        fine_modulation,
-        project_weight,
-        query_gain[None],
-        key_gain[None],
-        text_keys,
-        text_values,
-        output_weight,
-    )
-    return guided, fine.reshape(2, 1, 4096), hidden.reshape(2, 1, 128, 2048)
+        step_index, guide_index, text_length, project_weight, output_weight.T, *stored
+    )
+    return guided, fine, hidden.reshape(2, 1, 128, 2048)
 
 
 def solution(mesh):

time: 68.9 us -> 55.7 us (0.81)
  Pallas kernels: 56.3 us -> 48.5 us
  local copies, waits for them, and re-layouts: 9.42 us -> 4.25 us
    pallas_call x1, Pallas kernels: 56.3 us -> 48.5 us  [per_device(): pl.pallas_call(kernel, out_shape=(jax.ShapeDtypeStruct((2, 2048), f32), j...]
    unnamed x32 -> x5, local copies, waits for them, and re-layouts: 9.42 us -> 4.25 us
where the time goes in v4:
time: 55.7 us; the launch traced here: 55.4 us
  Pallas kernels  48.5 us (87%)
  local copies, waits for them, and re-layouts  4.25 us (8%)
  between operations  2.59 us (5%)
    pallas_call x1, Pallas kernels, per_device(): pl.pallas_call(kernel, out_shape=(jax.ShapeDtypeStruct((2, 2048), f32), j...  48.5 us
    unnamed x5, local copies, waits for them, and re-layouts  4.25 us

profile of v4, /device:TPU:1, one launch (start us, length us, event | category | flops | bytes accessed | tf_op | source)
XLA Modules:
  0.0 55.4 jit_solution(10647668759042720932)
XLA Ops:
  2.6 48.5 %shard_map.202 = (f32[2,2048]{1,0:T(2,128)}, f32[2,1,4096]{2,1,0:T(1,128)}, bf16[256,2048]{1,0:T(8,128)(2,1)}) custom-call(s32[1]{0:T(128)S(6)} %copy.26.step_ref, s32[1]{0:T(128)S(6)} %copy.27.guide_ref, s32[1]{0:T(128)S(6)} %copy.28.length_ref, bf16[8,3072]{1,0:T(8,128)(2,1)} %weight_ref.1, bf16[8,1024]{1,0:T(8,128)(2,1)} %bitcast.17, ...), custom_call_target="tpu_custom_call" | custom-call | tf_op jit(solution)/shard_map/pallas_call | solution.py:563
  51.1 0.0 copy-start
  51.1 1.3 %copy.29 = f32[2,2048]{1,0:T(2,128)} copy(f32[2,2048]{1,0:T(2,128)} %get-tuple-element.15) | data formatting | bytes 32768
  52.5 0.0 copy-done
  52.5 0.6 %copy.30 = f32[2,1,4096]{2,1,0:T(1,128)} copy(f32[2,1,4096]{2,1,0:T(1,128)S(1)} %copy-done) | data formatting | bytes 65536
  53.1 2.3 %copy.31 = bf16[2,1,128,2048]{3,2,1,0:T(8,128)(2,1)} copy(bf16[2,1,128,2048]{3,2,1,0:T(8,128)(2,1)} %bitcast.13) | data formatting | bytes 2097152
Async XLA Ops:
  51.1 1.3 %copy-start = (f32[2,1,4096]{2,1,0:T(1,128)S(1)}, f32[2,1,4096]{2,1,0:T(1,128)}, u32[]{:S(2)}) copy-start(f32[2,1,4096]{2,1,0:T(1,128)} %get-tuple-element.16) | copy-start | bytes 98308

commit v5 on v4

--- a/solution.py
+++ b/solution.py
@@ -104,15 +104,16 @@
 
 
 def kernel(
-    step_ref, guide_ref, length_ref, weight_ref, output_ref, *refs
+    weight_ref, output_ref, *refs
 ):
-    stored, refs = refs[:14], refs[14:]
+    stored, scalars, refs = refs[:14], refs[14:17], refs[17:]
     (guided_out, fine_out, hidden_out), held, refs = refs[:3], refs[3:17], refs[17:]
     (
         embed_ref, modulation_ref, bias_ref, latent_ref, hidden_ref, coarse_mod_ref, final_ref,
         text_keys_ref, key_gain_ref, text_values_ref, scales_ref, up_ref, up_bias_ref,
         query_gain_ref,
     ) = held
+    step_ref, guide_ref, length_ref = scalars
     run(
         step_ref, guide_ref, length_ref, weight_ref, output_ref, stored, held,
         embed_ref, modulation_ref, bias_ref, latent_ref, hidden_ref, coarse_mod_ref, final_ref,
@@ -129,14 +130,14 @@
     left, own_rows, group_rows, partial, z_parts, y_parts, folded,
     out_chunk, out_sibling, out_rows,
     velocity, latents, cells, grid_cells, pairs, query_tokens, key_tokens,
-    centred_right, state_right, folded_right, shift_row,
+    key_left, centred_right, state_right, folded_right,
     query_buf, key_buf, value_buf, text_key_buf, text_value_buf, ones_buf, attended,
     *sems,
 ):
     (
         a_send, a_recv, rz_send, rz_recv, ry_send, ry_recv, gz_send, gz_recv, gx_send, gx_recv,
         s_send, s_recv, wz_send, wz_recv, wp_send, wp_recv, wq_send, wq_recv, ws_send, ws_recv,
-        v_send, v_recv, l_send, l_recv, load_sem,
+        v_send, v_recv, l_send, l_recv, gs_send, gs_recv, load_sem,
     ) = sems
     loads = [
         pltpu.make_async_copy(source, target, load_sem.at[i])
@@ -194,6 +195,19 @@
         [bias_centred * scale, modulation_ref[0:1, :], jnp.zeros((6, width), f32)], 0
     )
 
+    swap.wait()
+    mine, other = out_chunk[core], out_sibling[...]
+    first = core == 0
+    out_rows[core, place.x_lo, y, z, place.x_hi] = jnp.concatenate(
+        [jnp.where(first, mine, other), jnp.where(first, other, mine)], 0
+    ).astype(bf16)
+    along_z = []
+    for d in range(1, 8):
+        slot = out_rows.at[core, place.x_lo, y, z, place.x_hi]
+        copy = remote(slot, slot, wz_send.at[d], wz_recv.at[d], place.at(z=lax.rem(z + d, 8)))
+        copy.start()
+        along_z.append(copy)
+
     for copy in spread:
         copy.wait()
     column = pl.multiple_of(lax.div(place.line, 4) * 128, 128)
@@ -217,19 +231,6 @@
         copy.start()
         scatter.append(copy)
     z_parts[z] = partial[pl.ds(z * 2, 2)]
-
-    swap.wait()
-    mine, other = out_chunk[core], out_sibling[...]
-    first = core == 0
-    out_rows[core, place.x_lo, y, z, place.x_hi] = jnp.concatenate(
-        [jnp.where(first, mine, other), jnp.where(first, other, mine)], 0
-    ).astype(bf16)
-    along_z = []
-    for d in range(1, 8):
-        slot = out_rows.at[core, place.x_lo, y, z, place.x_hi]
-        copy = remote(slot, slot, wz_send.at[d], wz_recv.at[d], place.at(z=lax.rem(z + d, 8)))
-        copy.start()
-        along_z.append(copy)
 
     for load in loads[4:7]:
         load.wait()
@@ -435,62 +436,77 @@
             ]
     own_tokens = query_tokens[...].astype(bf16)
 
-    for copy in gather_z:
-        copy.wait()
-    gather_x = []
-    for d in range(1, 8):
-        slot = folded.at[member]
-        copy = remote(
-            slot, slot, gx_send.at[d], gx_recv.at[d],
-            place.member_device(lax.rem(member + d, 8)),
-        )
-        copy.start()
-        gather_x.append(copy)
-
     for e in range(1, 4):
         along_p[e - 1].wait()
         send_q(e)
         send_sibling(e, 0)
+    for copy in gather_z:
+        copy.wait()
+    gather_x, to_twin = [], []
+
+    def send_twin(d):
+        source = lax.rem(place.x + 4 - d, 4)
+        slot = folded.at[lax.rem(source, 2) * 4 + lax.div(source, 2) * 2 + core]
+        copy = remote(slot, slot, gs_send.at[d], gs_recv.at[d], sibling)
+        copy.start()
+        to_twin.append(copy)
+
+    for d in range(1, 4):
+        slot = folded.at[member]
+        copy = remote(
+            slot, slot, gx_send.at[d], gx_recv.at[d], place.at(x=lax.rem(place.x + d, 4))
+        )
+        copy.start()
+        gather_x.append(copy)
+    send_twin(0)
+
     def rstd_of(tokens):
         centred = dot_nn(tokens, centred_right[...])
         return lax.rsqrt(jnp.mean(centred * centred, -1, keepdims=True) + epsilon)
 
-    query_rstd = rstd_of(own_tokens)
-    key_rstd = [rstd_of(key_tokens[row * 256 : row * 256 + 256, :]) for row in range(4)]
-
-    for copy in gather_x:
+    is_low = ((lane >= 32) & (lane < 64)) | (lane == 65)
+    is_one = (lane == 67) | (lane == 68)
+
+    def scaled(tokens):
+        high, low = split_two(rstd_of(tokens) * tokens.astype(f32))
+        return jnp.where(is_one, 1.0, jnp.where(is_low, low, high))
+
+    own_left = scaled(own_tokens).astype(bf16)
+    for row in range(4):
+        rows = slice(row * 256, row * 256 + 256)
+        key_left[rows, :] = (scaled(key_tokens[rows, :]) * row_ok[row]).astype(bf16)
+    folded_right[64:128, :] = jnp.zeros((64, 3072), bf16)
+
+    for d in range(1, 4):
+        gather_x[d - 1].wait()
+        send_twin(d)
+    for copy in to_twin:
         copy.wait()
     for part in range(8):
         for block in range(3):
             at = part * 384 + block * 128
-            folded_right[0:32, at : at + 128] = folded[part, block * 2 : block * 2 + 2].reshape(
-                32, 128
-            )
+            rows = folded[part, block * 2 : block * 2 + 2].reshape(32, 128)
+            folded_right[0:32, at : at + 128] = rows
+            folded_right[32:64, at : at + 128] = rows
             rest = folded[part, 6 + block // 2].astype(f32)[block % 2 * 8 : block % 2 * 8 + 8]
-            folded_right[32:80, at : at + 128] = jnp.concatenate(
-                [jnp.zeros((32, 128), f32), rest[0:1], rest[2:3], jnp.zeros((14, 128), f32)], 0
+            folded_right[64:80, at : at + 128] = jnp.concatenate(
+                [rest[0:1], rest[0:1], rest[2:3], rest[1:2], rest[3:4], jnp.zeros((11, 128), f32)],
+                0,
             ).astype(bf16)
-            folded_right[80:128, at : at + 128] = jnp.zeros((48, 128), bf16)
-            shift_row[:, at : at + 128] = rest[1:2] + rest[3:4]
-
-    def project(tokens, rstd, start):
-        cols = slice(start, start + 256)
-        return rstd * dot_nn(tokens, folded_right[:, cols]) + shift_row[:, cols]
+
+    def project(tokens, start):
+        return dot_nn(tokens, folded_right[:, start : start + 256])
 
     for pair in range(4):
         cols = slice(pair * 256, pair * 256 + 256)
-        query_buf[:, cols] = head_norm(project(own_tokens, query_rstd, pair * 256), query_gain)
+        query_buf[:, cols] = head_norm(project(own_left, pair * 256), query_gain)
     for row in range(4):
         rows = slice(row * 256, row * 256 + 256)
-        tokens = key_tokens[rows, :]
+        tokens = key_left[rows, :]
         for pair in range(4):
             cols = slice(pair * 256, pair * 256 + 256)
-            key_buf[rows, cols] = head_norm(
-                project(tokens, key_rstd[row], 1024 + pair * 256), key_gain
-            )
-            value_buf[rows, cols] = (
-                project(tokens, key_rstd[row], 2048 + pair * 256) * row_ok[row]
-            ).astype(bf16)
+            key_buf[rows, cols] = head_norm(project(tokens, 1024 + pair * 256), key_gain)
+            value_buf[rows, cols] = project(tokens, 2048 + pair * 256).astype(bf16)
 
     for head in range(HEADS):
         cols = slice(head * 128, head * 128 + 128)
@@ -520,6 +536,20 @@
             rows = out_rows[half, block // 4, block % 4].reshape(256, 512)
             output = output + dot_nt(attended[:, half * 512 : half * 512 + 512], rows)
         hidden_out[:, cols] = (total + modulation_ref[2:3, cols] * output).astype(bf16)
+
+
+def store_kernel(*refs):
+    copies = [
+        pltpu.make_async_copy(refs[i], refs[3 + i], refs[6].at[i]) for i in (2, 1, 0)
+    ]
+    for copy in copies:
+        copy.start()
+    for copy in copies:
+        copy.wait()
+
+
+def in_hbm(arrays):
+    return [pltpu.with_memory_space_constraint(array, pltpu.HBM) for array in arrays]
 
 
 def per_device(
@@ -545,21 +575,21 @@
 ):
     dma = pltpu.SemaphoreType.DMA
     sems = []
-    for shape in [(8,), (8,), (4,), (8,), (8,)]:
+    for shape in [(8,), (8,), (4,), (8,), (4,)]:
         sems += [dma(shape), dma(shape)]
     sems += [dma, dma]
-    for shape in [(8,), (4,), (4, 4), (4, 4), (5,), (2,)]:
+    for shape in [(8,), (4,), (4, 4), (4, 4), (5,), (2,), (4,)]:
         sems += [dma(shape), dma(shape)]
     sems += [dma((14,))]
     stored = [
         embed_weight, fine_modulation, embed_bias[None], coarse_latent,
         coarse_hidden.reshape(128, 2048), coarse_modulation[0], final_weight.T,
         text_keys, key_gain[None], text_values, guide_scales.reshape(32, 128),
-        upsample_weight.T, upsample_bias[None], query_gain[None],
+        upsample_weight.T, upsample_bias[None], query_gain[None], step_index, guide_index,
+        text_length,
     ]
     hbm = pl.BlockSpec(memory_space=pltpu.HBM)
     vmem = pl.BlockSpec(memory_space=pltpu.VMEM)
-    smem = pl.BlockSpec(memory_space=pltpu.SMEM)
     guided, fine, hidden = pl.pallas_call(
         kernel,
         out_shape=(
@@ -567,9 +597,9 @@
             jax.ShapeDtypeStruct((2, 1, 4096), f32),
             jax.ShapeDtypeStruct((256, 2048), bf16),
         ),
-        in_specs=[smem] * 3 + [vmem] * 2 + [hbm] * 14,
+        in_specs=[vmem] * 2 + [hbm] * 14 + [pl.BlockSpec(memory_space=pltpu.SMEM)] * 3,
         out_specs=(vmem, vmem, vmem),
-        scratch_shapes=[pltpu.VMEM(array.shape, array.dtype) for array in stored]
+        scratch_shapes=[pltpu.VMEM(array.shape, array.dtype) for array in stored[:14]]
         + [
             pltpu.VMEM((40, 2048), f32),
             pltpu.VMEM((8, 8, 384), f32),
@@ -588,10 +618,10 @@
             pltpu.VMEM((128, 64), f32),
             pltpu.VMEM((256, 128), f32),
             pltpu.VMEM((1024, 128), bf16),
+            pltpu.VMEM((1024, 128), bf16),
             pltpu.VMEM((128, 2048), bf16),
             pltpu.VMEM((128, 2048), bf16),
             pltpu.VMEM((128, 3072), bf16),
-            pltpu.VMEM((1, 3072), f32),
             pltpu.VMEM((256, 1024), bf16),
             pltpu.VMEM((1024, 1024), bf16),
             pltpu.VMEM((1024, 1024), bf16),
@@ -602,11 +632,19 @@
         ]
         + sems,
         compiler_params=pltpu.CompilerParams(
-            collective_id=0, has_side_effects=True, vmem_limit_bytes=56 * 1024 * 1024
+            collective_id=0, has_side_effects=True, vmem_limit_bytes=48 * 1024 * 1024
         ),
     )(
-        step_index, guide_index, text_length, project_weight, output_weight.T, *stored
-    )
+        *in_hbm([project_weight, output_weight.T]), *in_hbm(stored[:14]), *stored[14:]
+    )
+    results = (guided, fine, hidden)
+    guided, fine, hidden = pl.pallas_call(
+        store_kernel,
+        out_shape=[jax.ShapeDtypeStruct(array.shape, array.dtype) for array in results],
+        in_specs=[vmem] * 3,
+        out_specs=[hbm] * 3,
+        scratch_shapes=[dma((3,))],
+    )(*[pltpu.with_memory_space_constraint(array, pltpu.VMEM) for array in results])
     return guided, fine, hidden.reshape(2, 1, 128, 2048)
 
 

time: 55.7 us -> 58.2 us (1.045)
  Pallas kernels: 48.5 us -> 55.4 us
  local copies, waits for them, and re-layouts: 4.25 us -> 0 us
    pallas_call x1, Pallas kernels: 48.5 us -> 54.4 us  [per_device(): pl.pallas_call(kernel, out_shape=(jax.ShapeDtypeStruct((2, 2048), f32), j...]
    unnamed x5 -> x0, local copies, waits for them, and re-layouts: 4.25 us -> none
    pallas_call x0 -> x1, Pallas kernels: none -> 1 us  [per_device(): pl.pallas_call(store_kernel, out_shape=[jax.ShapeDtypeStruct(array.shape,...]
where the time goes in v5:
time: 58.2 us; the launch traced here: 58 us
  Pallas kernels  55.4 us (95%)
  between operations  2.58 us (4%)
    pallas_call x1, Pallas kernels, per_device(): pl.pallas_call(kernel, out_shape=(jax.ShapeDtypeStruct((2, 2048), f32), j...  54.4 us

profile of v5, /device:TPU:1, one launch (start us, length us, event | category | flops | bytes accessed | tf_op | source)
XLA Modules:
  0.0 58.0 jit_solution(8743433515777516795)
XLA Ops:
  2.6 54.4 %shard_map.202 = (f32[2,2048]{1,0:T(2,128)S(1)}, f32[2,1,4096]{2,1,0:T(1,128)S(1)}, bf16[256,2048]{1,0:T(8,128)(2,1)S(1)}) custom-call(bf16[8,3072]{1,0:T(8,128)(2,1)} %weight_ref.1, bf16[8,1024]{1,0:T(8,128)(2,1)} %bitcast.16, bf16[32,2048]{1,0:T(8,128)(2,1)} %refs_0_.1, f32[3,2048]{1,0:T(4,128)} %refs_1_.1, f32[1,2048]{1,0:T(1,128)} %bitcast.19, ...), custom_call_target="tpu_custom_call" | custom-call | tf_op jit(solution)/shard_map/pallas_call | solution.py:593
  57.0 1.0 %shard_map.203 = (f32[2,2048]{1,0:T(2,128)}, f32[2,1,4096]{2,1,0:T(1,128)}, bf16[256,2048]{1,0:T(8,128)(2,1)}) custom-call(f32[2,2048]{1,0:T(2,128)S(1)} %get-tuple-element.9.refs_0_, f32[2,1,4096]{2,1,0:T(1,128)S(1)} %get-tuple-element.10.refs_1_, bf16[256,2048]{1,0:T(8,128)(2,1)S(1)} %get-tuple-element.11.refs_2_), custom_call_target="tpu_custom_call" | custom-call | tf_op jit(solution)/shard_map/pallas_call | solution.py:641

commit v6 on v5

--- a/solution.py
+++ b/solution.py
@@ -195,19 +195,6 @@
         [bias_centred * scale, modulation_ref[0:1, :], jnp.zeros((6, width), f32)], 0
     )
 
-    swap.wait()
-    mine, other = out_chunk[core], out_sibling[...]
-    first = core == 0
-    out_rows[core, place.x_lo, y, z, place.x_hi] = jnp.concatenate(
-        [jnp.where(first, mine, other), jnp.where(first, other, mine)], 0
-    ).astype(bf16)
-    along_z = []
-    for d in range(1, 8):
-        slot = out_rows.at[core, place.x_lo, y, z, place.x_hi]
-        copy = remote(slot, slot, wz_send.at[d], wz_recv.at[d], place.at(z=lax.rem(z + d, 8)))
-        copy.start()
-        along_z.append(copy)
-
     for copy in spread:
         copy.wait()
     column = pl.multiple_of(lax.div(place.line, 4) * 128, 128)
@@ -232,6 +219,19 @@
         scatter.append(copy)
     z_parts[z] = partial[pl.ds(z * 2, 2)]
 
+    swap.wait()
+    mine, other = out_chunk[core], out_sibling[...]
+    first = core == 0
+    out_rows[core, place.x_lo, y, z, place.x_hi] = jnp.concatenate(
+        [jnp.where(first, mine, other), jnp.where(first, other, mine)], 0
+    ).astype(bf16)
+    along_z = []
+    for d in range(1, 8):
+        slot = out_rows.at[core, place.x_lo, y, z, place.x_hi]
+        copy = remote(slot, slot, wz_send.at[d], wz_recv.at[d], place.at(z=lax.rem(z + d, 8)))
+        copy.start()
+        along_z.append(copy)
+
     for load in loads[4:7]:
         load.wait()
     for row in range(2):
@@ -309,8 +309,6 @@
         copy.start()
         to_sibling.append(copy)
 
-    send_q(0)
-    send_sibling(0, 0)
 
     for load in loads[7:]:
         load.wait()
@@ -362,6 +360,9 @@
         copy = remote(slot, slot, gz_send.at[d], gz_recv.at[d], place.at(z=lax.rem(z + d, 8)))
         copy.start()
         gather_z.append(copy)
+
+    send_q(0)
+    send_sibling(0, 0)
 
     for copy in latent_copies + velocity_copies:
         copy.wait()
@@ -436,10 +437,6 @@
             ]
     own_tokens = query_tokens[...].astype(bf16)
 
-    for e in range(1, 4):
-        along_p[e - 1].wait()
-        send_q(e)
-        send_sibling(e, 0)
     for copy in gather_z:
         copy.wait()
     gather_x, to_twin = [], []
@@ -460,6 +457,10 @@
         gather_x.append(copy)
     send_twin(0)
 
+    for e in range(1, 4):
+        along_p[e - 1].wait()
+        send_q(e)
+        send_sibling(e, 0)
     def rstd_of(tokens):
         centred = dot_nn(tokens, centred_right[...])
         return lax.rsqrt(jnp.mean(centred * centred, -1, keepdims=True) + epsilon)

time: 58.2 us -> 50.9 us (0.87)
  Pallas kernels: 55.4 us -> 48.2 us
    pallas_call x1, Pallas kernels: 54.4 us -> 47.2 us  [per_device(): pl.pallas_call(kernel, out_shape=(jax.ShapeDtypeStruct((2, 2048), f32), j...]
where the time goes in v6:
time: 50.9 us; the launch traced here: 50.7 us
  Pallas kernels  48.2 us (95%)
  between operations  2.58 us (5%)
    pallas_call x1, Pallas kernels, per_device(): pl.pallas_call(kernel, out_shape=(jax.ShapeDtypeStruct((2, 2048), f32), j...  47.2 us

profile of v6, /device:TPU:1, one launch (start us, length us, event | category | flops | bytes accessed | tf_op | source)
XLA Modules:
  0.0 50.7 jit_solution(15386959273050985220)
XLA Ops:
  2.6 47.2 %shard_map.202 = (f32[2,2048]{1,0:T(2,128)S(1)}, f32[2,1,4096]{2,1,0:T(1,128)S(1)}, bf16[256,2048]{1,0:T(8,128)(2,1)S(1)}) custom-call(bf16[8,3072]{1,0:T(8,128)(2,1)} %weight_ref.1, bf16[8,1024]{1,0:T(8,128)(2,1)} %bitcast.16, bf16[32,2048]{1,0:T(8,128)(2,1)} %refs_0_.1, f32[3,2048]{1,0:T(4,128)} %refs_1_.1, f32[1,2048]{1,0:T(1,128)} %bitcast.19, ...), custom_call_target="tpu_custom_call" | custom-call | tf_op jit(solution)/shard_map/pallas_call | solution.py:594
  49.7 1.0 %shard_map.203 = (f32[2,2048]{1,0:T(2,128)}, f32[2,1,4096]{2,1,0:T(1,128)}, bf16[256,2048]{1,0:T(8,128)(2,1)}) custom-call(f32[2,2048]{1,0:T(2,128)S(1)} %get-tuple-element.9.refs_0_, f32[2,1,4096]{2,1,0:T(1,128)S(1)} %get-tuple-element.10.refs_1_, bf16[256,2048]{1,0:T(8,128)(2,1)S(1)} %get-tuple-element.11.refs_2_), custom_call_target="tpu_custom_call" | custom-call | tf_op jit(solution)/shard_map/pallas_call | solution.py:642

commit v7 on v6

--- a/solution.py
+++ b/solution.py
@@ -130,7 +130,7 @@
     left, own_rows, group_rows, partial, z_parts, y_parts, folded,
     out_chunk, out_sibling, out_rows,
     velocity, latents, cells, grid_cells, pairs, query_tokens, key_tokens,
-    key_left, centred_right, state_right, folded_right,
+    key_left, centred_right, state_right, folded_right, state,
     query_buf, key_buf, value_buf, text_key_buf, text_value_buf, ones_buf, attended,
     *sems,
 ):
@@ -477,6 +477,9 @@
         rows = slice(row * 256, row * 256 + 256)
         key_left[rows, :] = (scaled(key_tokens[rows, :]) * row_ok[row]).astype(bf16)
     folded_right[64:128, :] = jnp.zeros((64, 3072), bf16)
+    for block in range(8):
+        cols = slice(block * 256, block * 256 + 256)
+        state[:, cols] = dot_nn(own_tokens, state_right[:, cols])
 
     for d in range(1, 4):
         gather_x[d - 1].wait()
@@ -522,8 +525,8 @@
             attended[row * 128 : row * 128 + 128, cols] = (sums[:, :128] / sums[:, 128:]).astype(
                 bf16
             )
-        if head >= 2:
-            for item in range((head - 2) * 2, (head - 2) * 2 + 2):
+        if head >= 5:
+            for item in range((head - 5) * 4, (head - 5) * 4 + 4):
                 along_q[item].wait()
                 send_sibling(item // 3, item % 3 + 1)
 
@@ -531,12 +534,11 @@
         copy.wait()
     for block in range(8):
         cols = slice(block * 256, block * 256 + 256)
-        total = dot_nn(own_tokens, state_right[:, cols])
         output = jnp.zeros((256, 256), f32)
         for half in range(2):
             rows = out_rows[half, block // 4, block % 4].reshape(256, 512)
             output = output + dot_nt(attended[:, half * 512 : half * 512 + 512], rows)
-        hidden_out[:, cols] = (total + modulation_ref[2:3, cols] * output).astype(bf16)
+        hidden_out[:, cols] = (state[:, cols] + modulation_ref[2:3, cols] * output).astype(bf16)
 
 
 def store_kernel(*refs):
@@ -623,6 +625,7 @@
             pltpu.VMEM((128, 2048), bf16),
             pltpu.VMEM((128, 2048), bf16),
             pltpu.VMEM((128, 3072), bf16),
+            pltpu.VMEM((256, 2048), f32),
             pltpu.VMEM((256, 1024), bf16),
             pltpu.VMEM((1024, 1024), bf16),
             pltpu.VMEM((1024, 1024), bf16),

time: 50.9 us -> 50.2 us (0.986)
  Pallas kernels: 48.2 us -> 47.4 us
    pallas_call x1, Pallas kernels: 47.2 us -> 46.4 us  [per_device(): pl.pallas_call(kernel, out_shape=(jax.ShapeDtypeStruct((2, 2048), f32), j...]
where the time goes in v7:
time: 50.2 us; the launch traced here: 50 us
  Pallas kernels  47.4 us (94%)
  between operations  2.58 us (5%)
    pallas_call x1, Pallas kernels, per_device(): pl.pallas_call(kernel, out_shape=(jax.ShapeDtypeStruct((2, 2048), f32), j...  46.4 us

profile of v7, /device:TPU:1, one launch (start us, length us, event | category | flops | bytes accessed | tf_op | source)
XLA Modules:
  0.0 50.0 jit_solution(5689817394405258208)
XLA Ops:
  2.6 46.4 %shard_map.202 = (f32[2,2048]{1,0:T(2,128)S(1)}, f32[2,1,4096]{2,1,0:T(1,128)S(1)}, bf16[256,2048]{1,0:T(8,128)(2,1)S(1)}) custom-call(bf16[8,3072]{1,0:T(8,128)(2,1)} %weight_ref.1, bf16[8,1024]{1,0:T(8,128)(2,1)} %bitcast.16, bf16[32,2048]{1,0:T(8,128)(2,1)} %refs_0_.1, f32[3,2048]{1,0:T(4,128)} %refs_1_.1, f32[1,2048]{1,0:T(1,128)} %bitcast.19, ...), custom_call_target="tpu_custom_call" | custom-call | tf_op jit(solution)/shard_map/pallas_call | solution.py:596
  49.0 1.0 %shard_map.203 = (f32[2,2048]{1,0:T(2,128)}, f32[2,1,4096]{2,1,0:T(1,128)}, bf16[256,2048]{1,0:T(8,128)(2,1)}) custom-call(f32[2,2048]{1,0:T(2,128)S(1)} %get-tuple-element.9.refs_0_, f32[2,1,4096]{2,1,0:T(1,128)S(1)} %get-tuple-element.10.refs_1_, bf16[256,2048]{1,0:T(8,128)(2,1)S(1)} %get-tuple-element.11.refs_2_), custom_call_target="tpu_custom_call" | custom-call | tf_op jit(solution)/shard_map/pallas_call | solution.py:645

commit v8 on v7

--- a/solution.py
+++ b/solution.py
@@ -198,11 +198,15 @@
     for copy in spread:
         copy.wait()
     column = pl.multiple_of(lax.div(place.line, 4) * 128, 128)
-    total = jnp.dot(
-        left[:, pl.ds(column, 128)], group_rows[0].reshape(128, 384), precision=highest
-    ) + jnp.dot(
-        left[:, pl.ds(1024 + column, 128)], group_rows[1].reshape(128, 384), precision=highest
-    )
+    total = jnp.zeros((40, 384), f32)
+    for half in range(2):
+        high, rest = split_two(left[:, pl.ds(half * 1024 + column, 128)])
+        middle, low = split_two(rest)
+        terms = dot_nn(
+            jnp.concatenate([high, middle, low], 0).astype(bf16),
+            group_rows[half].reshape(128, 384).astype(bf16),
+        )
+        total = total + (terms[:40] + terms[40:80] + terms[80:])
     for row in range(5):
         for block in range(3):
             place_at = block * 4 + row if row < 4 else 12 + block
@@ -515,16 +519,22 @@
     for head in range(HEADS):
         cols = slice(head * 128, head * 128 + 128)
         text_right = jnp.concatenate([text_value_buf[:, cols], ones_buf[1024:1280, :]], 1)
-        for row in range(2):
-            window = slice(row * 256, row * 256 + 768)
-            query = query_buf[row * 128 : row * 128 + 128, cols]
-            weights = jnp.exp2(dot_nt(query, key_buf[window, cols])).astype(bf16)
-            text_weights = jnp.exp2(dot_nt(query, text_key_buf[:, cols])).astype(bf16)
+        query = query_buf[:, cols]
+
+        def weighted(part, window):
+            weights = jnp.exp2(dot_nt(part, key_buf[window, cols])).astype(bf16)
             right = jnp.concatenate([value_buf[window, cols], ones_buf[window, :]], 1)
-            sums = dot_nn(weights, right) + dot_nn(text_weights, text_right)
-            attended[row * 128 : row * 128 + 128, cols] = (sums[:, :128] / sums[:, 128:]).astype(
-                bf16
+            return dot_nn(weights, right)
+
+        text_weights = jnp.exp2(dot_nt(query, text_key_buf[:, cols])).astype(bf16)
+        sums = (
+            weighted(query, slice(256, 768))
+            + dot_nn(text_weights, text_right)
+            + jnp.concatenate(
+                [weighted(query[:128], slice(0, 256)), weighted(query[128:], slice(768, 1024))], 0
             )
+        )
+        attended[:, cols] = (sums[:, :128] / sums[:, 128:]).astype(bf16)
         if head >= 5:
             for item in range((head - 5) * 4, (head - 5) * 4 + 4):
                 along_q[item].wait()

time: 50.2 us -> 50.1 us (level)
  no operation moved by 1% of the time
where the time goes in v8:
time: 50.1 us; the launch traced here: 49.9 us
  Pallas kernels  47.3 us (94%)
  between operations  2.58 us (5%)
    pallas_call x1, Pallas kernels, per_device(): pl.pallas_call(kernel, out_shape=(jax.ShapeDtypeStruct((2, 2048), f32), j...  46.3 us

profile of v8, /device:TPU:1, one launch (start us, length us, event | category | flops | bytes accessed | tf_op | source)
XLA Modules:
  0.0 49.9 jit_solution(2452536290684933322)
XLA Ops:
  2.6 46.3 %shard_map.202 = (f32[2,2048]{1,0:T(2,128)S(1)}, f32[2,1,4096]{2,1,0:T(1,128)S(1)}, bf16[256,2048]{1,0:T(8,128)(2,1)S(1)}) custom-call(bf16[8,3072]{1,0:T(8,128)(2,1)} %weight_ref.1, bf16[8,1024]{1,0:T(8,128)(2,1)} %bitcast.16, bf16[32,2048]{1,0:T(8,128)(2,1)} %refs_0_.1, f32[3,2048]{1,0:T(4,128)} %refs_1_.1, f32[1,2048]{1,0:T(1,128)} %bitcast.19, ...), custom_call_target="tpu_custom_call" | custom-call | tf_op jit(solution)/shard_map/pallas_call | solution.py:606
  48.9 1.0 %shard_map.203 = (f32[2,2048]{1,0:T(2,128)}, f32[2,1,4096]{2,1,0:T(1,128)}, bf16[256,2048]{1,0:T(8,128)(2,1)}) custom-call(f32[2,2048]{1,0:T(2,128)S(1)} %get-tuple-element.9.refs_0_, f32[2,1,4096]{2,1,0:T(1,128)S(1)} %get-tuple-element.10.refs_1_, bf16[256,2048]{1,0:T(8,128)(2,1)S(1)} %get-tuple-element.11.refs_2_), custom_call_target="tpu_custom_call" | custom-call | tf_op jit(solution)/shard_map/pallas_call | solution.py:655
